TPU v7x, 128 devices: a whole 4x4x4 slice. The times are simulated.
128 devices in a mesh: dp: 8 (over x, y_lo), tensor: 16 (over y_hi, z, core).
Axes of the slice: x: 4, y: 4 (y_hi: 2, y_lo: 2; y = y_hi * 2 + y_lo), z: 4, core: 2. Of those that a mesh axis runs over, the one named last changes fastest.
Arguments:
- hidden_in: bfloat16 [2048, 8192], P('dp', 'tensor'), may hold values from -6 to 6
- norm_gain: float32 [8192], replicated, may hold values from 0.5 to 1.5
- clip_base: float32 [8192], replicated, may hold values from 0.5 to 2
- pct_index: int32 [8192], replicated, may hold values from 0 to 63
- clip_step: float32 [8192], replicated, may hold values from -4 to 4
- w_query: bfloat16 [8192, 8192], P(None, 'tensor'), may hold values from -1 to 1
- w_key: bfloat16 [8192, 1024], P(None, 'tensor'), may hold values from -1 to 1
- w_value: bfloat16 [8192, 1024], P(None, 'tensor'), may hold values from -0.0625 to 0.0625
- w_out: bfloat16 [8192, 8192], P('tensor'), may hold values from -0.0625 to 0.0625
- doc_ids: int32 [8, 256], P('dp'), may hold values from 0 to 3, never falling along the last dimension, each value on 1 to 128 neighbouring positions
Outputs:
- tangent_out: bfloat16 [2048, 8192], P('dp', 'tensor')
- gn_product: float32 [8192], P('tensor')
Inputs may be any that keep to these rules, and one draw needn't show every extreme that they name: `doc_ids`: document numbers never fall along a sequence; each document holds 1 to 128 positions.
All inputs are finite; a program needn't handle non-finite values.
Results may differ from a plain program's by a relative error of at most 0.02.
The roundings to bfloat16 on the way count: a program that leaves them out, or rounds other values in their place, can miss the bound.
Values may be sent and summed in bfloat16 or wider, within the bound.
A program may use at most 128 MiB of HBM per device.

v0:
```python
import math

import jax
import jax.numpy as jnp
from jax import lax
from jax.sharding import PartitionSpec as P

HEAD_DIM = 128


EPSILON = 1e-05
ROPE_BASE = 500000.0
MASKED = -1e30


def rope_tables(token_count, head_size):
    positions = jnp.arange(token_count, dtype=jnp.float32)
    frequency = jnp.exp(
        -math.log(ROPE_BASE) * 2.0 * jnp.arange(head_size // 2, dtype=jnp.float32) / head_size
    )
    angles = positions[:, None] * frequency[None, :]
    return (jnp.cos(angles)[:, None, :], jnp.sin(angles)[:, None, :])


def rotate(values, cosine, sine_part, turning):
    half_dim = values.shape[-1] // 2
    front_part = values[..., :half_dim]
    back_part = values[..., half_dim:]
    return jnp.concatenate(
        [
            front_part * cosine - turning * back_part * sine_part,
            back_part * cosine + turning * front_part * sine_part,
        ],
        axis=-1,
    )


def contract_last(left_side, right_side):
    return lax.dot_general(
        left_side, right_side, (((1,), (1,)), ((), ())), preferred_element_type=jnp.float32
    )


def on_device(
    hidden_in, norm_gain, clip_base, pct_index, clip_step, w_query, w_key, w_value, w_out, doc_ids
):
    f32 = jnp.float32
    bf16 = jnp.bfloat16
    token_count, shard_width = hidden_in.shape
    tensor_count = lax.axis_size("tensor")
    width = shard_width * tensor_count
    tensor_rank = lax.axis_index("tensor")
    offset = tensor_rank * shard_width
    thresh = clip_base * (1.0 + pct_index.astype(f32) / 32.0)
    local_heads = w_query.shape[1] // HEAD_DIM
    key_width = w_key.shape[1] * tensor_count
    key_heads = key_width // HEAD_DIM
    head_group = local_heads * tensor_count // key_heads
    key_head = tensor_rank * local_heads // head_group
    score_scale = HEAD_DIM ** (-0.5)

    def shard_slice(vector):
        return lax.dynamic_slice_in_dim(vector, offset, shard_width)

    rows_float = hidden_in.astype(f32)
    square_total = lax.psum(jnp.sum(rows_float * rows_float, axis=1), "tensor")
    normed = (
        rows_float * lax.rsqrt(square_total / width + EPSILON)[:, None] * shard_slice(norm_gain)
    )
    thresh_part = shard_slice(thresh)
    ratios = normed / thresh_part
    bent_vals = jnp.tanh(ratios)
    clipped_part = (thresh_part * bent_vals).astype(bf16)
    slopes = bent_vals - ratios * (1.0 - bent_vals * bent_vals)
    tangent_part = (slopes * shard_slice(clip_step)).astype(bf16)
    clipped, tangent = (
        lax.all_gather(clipped_part, "tensor", axis=1, tiled=True),
        lax.all_gather(tangent_part, "tensor", axis=1, tiled=True),
    )
    stacked = jnp.concatenate([clipped, tangent], axis=0)
    cosine, sine_part = rope_tables(token_count, HEAD_DIM)
    query_both = jnp.dot(stacked, w_query, preferred_element_type=f32).reshape(
        2 * token_count, local_heads, HEAD_DIM
    )
    query_p = rotate(query_both[:token_count], cosine, sine_part, 1.0).astype(bf16)
    query_t = rotate(query_both[token_count:], cosine, sine_part, 1.0).astype(bf16)
    key_raw = jnp.dot(stacked, w_key, preferred_element_type=f32).astype(bf16)
    value_raw = jnp.dot(stacked, w_value, preferred_element_type=f32).astype(bf16)
    key_all, value_all = (
        lax.all_gather(key_raw, "tensor", axis=1, tiled=True),
        lax.all_gather(value_raw, "tensor", axis=1, tiled=True),
    )
    key_mine = lax.dynamic_slice_in_dim(
        key_all.reshape(2 * token_count, HEAD_DIM, key_heads), key_head, 1, 2
    )[:, :, 0].astype(f32)
    value_mine = lax.dynamic_slice_in_dim(
        value_all.reshape(2 * token_count, HEAD_DIM, key_heads), key_head, 1, 2
    )[:, :, 0]
    key_p = rotate(key_mine[:token_count][:, None, :], cosine, sine_part, 1.0)[:, 0, :].astype(bf16)
    key_t = rotate(key_mine[token_count:][:, None, :], cosine, sine_part, 1.0)[:, 0, :].astype(bf16)
    value_p = value_mine[:token_count]
    value_t = value_mine[token_count:]
    doc_row = doc_ids[0]
    places = jnp.arange(token_count)
    allowed = (doc_row[:, None] == doc_row[None, :]) & (places[:, None] >= places[None, :])
    scores = jnp.einsum("shd,td->hst", query_p, key_p, preferred_element_type=f32) * score_scale
    attn_probs = jax.nn.softmax(jnp.where(allowed[None], scores, MASKED), axis=-1)
    probs_b = attn_probs.astype(bf16)
    tan_scores = (
        jnp.einsum("shd,td->hst", query_t, key_p, preferred_element_type=f32)
        + jnp.einsum("shd,td->hst", query_p, key_t, preferred_element_type=f32)
    ) * score_scale
    tan_probs = (
        attn_probs * (tan_scores - jnp.sum(attn_probs * tan_scores, axis=-1, keepdims=True))
    ).astype(bf16)
    tan_ctx = (
        jnp.einsum("hst,td->shd", tan_probs, value_p, preferred_element_type=f32)
        + jnp.einsum("hst,td->shd", probs_b, value_t, preferred_element_type=f32)
    ).astype(bf16)
    tan_ctx = tan_ctx.reshape(token_count, local_heads * HEAD_DIM)
    partial_out = jnp.dot(tan_ctx, w_out, preferred_element_type=f32)
    tangent_shard = (
        lax.psum_scatter(
            partial_out.astype(jnp.bfloat16), "tensor", scatter_dimension=1, tiled=True
        )
        .astype(jnp.float32)
        .astype(bf16)
    )
    back_ctx = contract_last(lax.all_gather(tangent_shard, "tensor", axis=1, tiled=True), w_out)
    back_ctx = back_ctx.astype(bf16).reshape(token_count, local_heads, HEAD_DIM)
    grad_prob = jnp.einsum("shd,td->hst", back_ctx, value_p, preferred_element_type=f32)
    grad_score = (
        attn_probs
        * (grad_prob - jnp.sum(attn_probs * grad_prob, axis=-1, keepdims=True))
        * score_scale
    ).astype(bf16)
    grad_query = (
        rotate(
            jnp.einsum("hst,td->shd", grad_score, key_p, preferred_element_type=f32),
            cosine,
            sine_part,
            -1.0,
        )
        .astype(bf16)
        .reshape(token_count, local_heads * HEAD_DIM)
    )
    key_local = jnp.sum(
        rotate(
            jnp.einsum("hst,shd->thd", grad_score, query_p, preferred_element_type=f32),
            cosine,
            sine_part,
            -1.0,
        ),
        axis=1,
    )
    value_local = jnp.einsum("hst,shd->td", probs_b, back_ctx, preferred_element_type=f32)
    selector = (jnp.arange(key_heads) == key_head).astype(f32)
    key_placed = (key_local.astype(bf16).astype(f32)[:, :, None] * selector).reshape(
        token_count, key_width
    )
    value_placed = (value_local.astype(bf16).astype(f32)[:, :, None] * selector).reshape(
        token_count, key_width
    )
    grad_key, grad_value = (
        lax.psum_scatter(
            key_placed.astype(jnp.bfloat16), "tensor", scatter_dimension=1, tiled=True
        ).astype(jnp.float32),
        lax.psum_scatter(
            value_placed.astype(jnp.bfloat16), "tensor", scatter_dimension=1, tiled=True
        ).astype(jnp.float32),
    )
    partial_in = (
        contract_last(grad_query, w_query)
        + contract_last(grad_key.astype(bf16), w_key)
        + contract_last(grad_value.astype(bf16), w_value)
    )
    token_total = token_count * lax.axis_size("dp")
    grad_shard = lax.psum_scatter(
        partial_in.astype(jnp.bfloat16), "tensor", scatter_dimension=1, tiled=True
    ).astype(jnp.float32)
    channel = jnp.sum(grad_shard * slopes, axis=0) / token_total
    gn_product = lax.psum(channel, "dp")
    return (tangent_shard, gn_product)


def solution(mesh):
    in_specs = (
        P("dp", "tensor"),
        P(),
        P(),
        P(),
        P(),
        P(None, "tensor"),
        P(None, "tensor"),
        P(None, "tensor"),
        P("tensor", None),
        P("dp", None),
    )
    out_specs = (P("dp", "tensor"), P("tensor"))
    return jax.shard_map(
        on_device, mesh=mesh, in_specs=in_specs, out_specs=out_specs, check_vma=False
    )
```

profile of v0, /device:TPU:0, one launch (start us, length us, event | category | flops | bytes accessed | tf_op | source)
XLA Modules:
  0.0 683.5 jit_solution(14804712984854762105)
XLA Ops:
  8.8 1.1 fusion.23
  9.9 39.3 %psum.14 = f32[256]{0:T(256)S(1)} all-reduce(f32[256]{0:T(256)S(1)} %fusion.23), channel_id=1, replica_groups=mesh['dp'=8,'tensor'=16] {'tensor'}, use_global_device_ids=true, to_apply=%region_1.2 | all-reduce | flops 256 | bytes 2048 | tf_op jit(solution)/shard_map/psum | solution.py:66
  50.0 2.0 multiply_convert_fusion.2
  52.9 1.5 fusion.39
  54.4 1.2 broadcast_multiply_fusion
  55.6 50.3 %all-gather.6.cloned.1.call-done = bf16[256,8192]{1,0:T(8,128)(2,1)} async-done(((bf16[256,512]{1,0:T(8,128)(2,1)}), bf16[256,8192]{1,0:T(8,128)(2,1)}) %all-gather.6.cloned.1.call-update) | async-done | bytes 4194320 | tf_op jit(solution)/shard_map/all_gather | solution.py:77
  105.9 4.5 constant_dynamic-update-slice_fusion.1
  110.4 52.8 %all-gather.8.cloned.1.call-done = bf16[256,8192]{1,0:T(8,128)(2,1)} async-done(((bf16[256,512]{1,0:T(8,128)(2,1)}), bf16[256,8192]{1,0:T(8,128)(2,1)}) %all-gather.8.cloned.1.call-update) | async-done | bytes 4194320 | tf_op jit(solution)/shard_map/all_gather | solution.py:78
  163.2 4.6 constant_dynamic-update-slice_fusion
  167.8 6.7 convolution_convert_fusion.2
  174.6 9.5 %fusion.66 = f32[512,512]{0,1:T(8,128)S(1)} fusion(bf16[512,8192]{1,0:T(8,128)(2,1)} %constant_dynamic-update-slice_fusion, bf16[8192,512]{1,0:T(8,128)(2,1)} %param.15), kind=kOutput, calls=%fused_computation.124 | convolution fusion | flops 4294967296 | bytes 17825792 | tf_op jit(solution)/shard_map/dot_general | solution.py:82
  184.2 6.7 convolution_convert_fusion.3
  191.9 1.1 copy.82
  193.0 1.0 copy.83
  194.8 1.2 copy.84
  195.9 1.0 copy.85
  197.0 2.2 subtract_convert_fusion.2
  199.2 0.9 pad_maximum_fusion
  200.1 17.1 %all-gather.12.cloned.1.call-done = bf16[512,1024]{0,1:T(8,128)(2,1)} async-done(((bf16[512,64]{0,1:T(8,128)(2,1)}), bf16[512,1024]{0,1:T(8,128)(2,1)}) %all-gather.12.cloned.1.call-update) | async-done | bytes 1048592 | tf_op jit(solution)/shard_map/all_gather | solution.py:90
  217.2 1.5 constant_dynamic-slice_fusion.1
  219.0 1.2 subtract_convert_fusion.3
  220.9 1.3 fusion.33
  222.2 2.4 fusion.65
  224.6 38.5 %all-gather.10.cloned.1.call-done = bf16[512,1024]{0,1:T(8,128)(2,1)} async-done(((bf16[512,64]{0,1:T(8,128)(2,1)}), bf16[512,1024]{0,1:T(8,128)(2,1)}) %all-gather.10.cloned.1.call-update) | async-done | bytes 1048592 | tf_op jit(solution)/shard_map/all_gather | solution.py:91
  263.2 1.6 constant_dynamic-slice_fusion.2
  264.7 3.3 multiply_reduce_fusion
  268.1 2.1 fusion.26
  270.2 1.7 fusion.13
  271.8 7.7 %convolution_convert_fusion = bf16[256,8192]{1,0:T(8,128)(2,1)} fusion(bf16[256,512]{0,1:T(8,128)(2,1)S(1)} %bitcast.110, bf16[512,8192]{1,0:T(8,128)(2,1)} %param.18), kind=kOutput, calls=%fused_computation.5 | convolution fusion | flops 2149580800 | bytes 12845056 | tf_op jit(solution)/shard_map/dot_general | solution.py:121
  279.6 79.4 %reduce-scatter.5.cloned.1.call-done = bf16[256,512]{1,0:T(8,128)(2,1)} async-done(((bf16[256,8192]{1,0:T(8,128)(2,1)}), bf16[256,512]{1,0:T(8,128)(2,1)}) %reduce-scatter.5.cloned.1.call-update) | async-done | bytes 262160 | tf_op jit(solution)/shard_map/reduce_scatter | solution.py:123
  359.4 58.2 %all-gather.14.cloned.1.call-done = bf16[256,8192]{1,0:T(8,128)(2,1)} async-done(((bf16[256,512]{1,0:T(8,128)(2,1)}), bf16[256,8192]{1,0:T(8,128)(2,1)}) %all-gather.14.cloned.1.call-update) | async-done | bytes 4194320 | tf_op jit(solution)/shard_map/all_gather | solution.py:129
  417.6 7.0 %fusion.14 = bf16[32,4,8,128]{3,2,1,0:T(8,128)(2,1)S(1)} fusion(bf16[256,8192]{1,0:T(8,128)(2,1)} %all-gather.14.cloned.1.call-done, bf16[512,8192]{1,0:T(8,128)(2,1)} %param.18), kind=kOutput, calls=%fused_computation.24 | convolution fusion | flops 2147614720 | bytes 12845056 | tf_op jit(solution)/shard_map/dot_general | solution.py:39
  424.6 1.3 convolution_bitcast_fusion
  426.0 2.8 convolution_bitcast_fusion.2
  428.7 2.7 convolution_bitcast_fusion.1
  431.4 2.4 fusion.16
  433.9 1.9 multiply_subtract_fusion
  436.1 1.0 copy.67
  437.1 1.3 fusion.17
  438.5 1.1 pad_maximum_fusion.1
  439.8 9.0 %fusion.67 = f32[256,8192]{1,0:T(8,128)} fusion(bf16[256,512]{0,1:T(8,128)(2,1)S(1)} %bitcast.109, bf16[8192,512]{1,0:T(8,128)(2,1)} %param.15), kind=kOutput, calls=%fused_computation.125 | convolution fusion | flops 2147483648 | bytes 17039360 | tf_op jit(solution)/shard_map/dot_general | solution.py:39
  448.8 52.9 %reduce-scatter.7.cloned.1.call-done = bf16[256,64]{0,1:T(8,128)(2,1)} async-done(((bf16[256,1024]{0,1:T(8,128)(2,1)}), bf16[256,64]{0,1:T(8,128)(2,1)}) %reduce-scatter.7.cloned.1.call-update) | async-done | bytes 32784 | tf_op jit(solution)/shard_map/reduce_scatter | solution.py:165
  501.7 7.9 %convolution_add_fusion.1 = f32[256,8192]{1,0:T(8,128)} fusion(f32[256,8192]{1,0:T(8,128)} %fusion.67, bf16[256,64]{0,1:T(8,128)(2,1)} %reduce-scatter.7.cloned.1.call-done, bf16[8192,64]{0,1:T(8,128)(2,1)S(1)} %copy-done), kind=kOutput, calls=%fused_computation.3 | convolution fusion | flops 270532608 | bytes 17858560 | tf_op jit(solution)/shard_map/dot_general | solution.py:39
  509.6 60.4 %reduce-scatter.9.cloned.1.call-done = bf16[256,64]{0,1:T(8,128)(2,1)} async-done(((bf16[256,1024]{0,1:T(8,128)(2,1)}), bf16[256,64]{0,1:T(8,128)(2,1)}) %reduce-scatter.9.cloned.1.call-update) | async-done | bytes 32784 | tf_op jit(solution)/shard_map/reduce_scatter | solution.py:168
  570.0 6.7 fusion.2
  576.7 79.8 %reduce-scatter.11.cloned.1.call-done = bf16[256,512]{1,0:T(8,128)(2,1)} async-done(((bf16[256,8192]{1,0:T(8,128)(2,1)}), bf16[256,512]{1,0:T(8,128)(2,1)}) %reduce-scatter.11.cloned.1.call-update) | async-done | bytes 262160 | tf_op jit(solution)/shard_map/reduce_scatter | solution.py:178
  656.5 1.2 multiply_reduce_fusion.2
  657.8 19.2 %psum.15 = f32[512]{0:T(512)} all-reduce(f32[512]{0:T(512)S(1)} %broadcast_multiply_fusion.1), channel_id=1, replica_groups=mesh['dp'=8,'tensor'=16] {'dp'}, use_global_device_ids=true, to_apply=%region_12.13 | all-reduce | flops 512 | bytes 4096 | tf_op jit(solution)/shard_map/psum | solution.py:182
  (55 shorter events, 7.1 us)
Async XLA Ops:
  7.2 160.7 %copy-start = (bf16[8192,64]{0,1:T(8,128)(2,1)S(1)}, bf16[8192,64]{0,1:T(8,128)(2,1)}, u32[]{:S(2)}) copy-start(bf16[8192,64]{0,1:T(8,128)(2,1)} %param.16) | copy-start | bytes 3145732
  7.2 98.7 %all-gather.6.cloned.1.call-start = ((), (), s32[]{:S(2)}) async-start(), calls=%async_computation.4 | async-start | bytes 4456448 | tf_op jit(solution)/shard_map/all_gather | solution.py:77
  52.1 111.2 %all-gather.8.cloned.1.call-start = ((), (), s32[]{:S(2)}) async-start(), calls=%async_computation.5 | async-start | bytes 4456448 | tf_op jit(solution)/shard_map/all_gather | solution.py:78
  52.8 164.4 %all-gather.12.cloned.1.call-start = ((), (), s32[]{:S(2)}) async-start(), calls=%async_computation.7 | async-start | bytes 1114112 | tf_op jit(solution)/shard_map/all_gather | solution.py:90
  174.5 9.7 %copy-start.1 = (bf16[8192,64]{0,1:T(8,128)(2,1)S(1)}, bf16[8192,64]{0,1:T(8,128)(2,1)}, u32[]{:S(2)}) copy-start(bf16[8192,64]{0,1:T(8,128)(2,1)} %param.17) | copy-start | bytes 3145732
  174.5 88.6 %all-gather.10.cloned.1.call-start = ((), (), s32[]{:S(2)}) async-start(), calls=%async_computation.6 | async-start | bytes 1114112 | tf_op jit(solution)/shard_map/all_gather | solution.py:91
  190.9 168.1 %reduce-scatter.5.cloned.1.call-start = ((), (), s32[]{:S(2)}) async-start(), calls=%async_computation.8 | async-start | bytes 4456448 | tf_op jit(solution)/shard_map/reduce_scatter | solution.py:123
  220.3 0.6 copy-start.4
  224.6 54.9 %copy-start.7 = (f32[4,256]{1,0:T(4,128)}, f32[4,256]{1,0:T(4,128)S(1)}, u32[]{:S(2)}) copy-start(f32[4,256]{1,0:T(4,128)S(1)} %get-tuple-element.37) | copy-start | bytes 12292
  279.6 138.0 %all-gather.14.cloned.1.call-start = ((), (), s32[]{:S(2)}) async-start(), calls=%async_computation.9 | async-start | bytes 4456448 | tf_op jit(solution)/shard_map/all_gather | solution.py:129
  359.0 142.7 %reduce-scatter.7.cloned.1.call-start = ((), (), s32[]{:S(2)}) async-start(), calls=%async_computation.10 | async-start | bytes 557056 | tf_op jit(solution)/shard_map/reduce_scatter | solution.py:165
  359.4 66.5 %copy-start.5 = (bf16[256,128,1]{1,0,2:T(8,128)(2,1)S(1)}, bf16[256,128,1]{1,0,2:T(8,128)(2,1)}, u32[]{:S(2)}) copy-start(bf16[256,128,1]{1,0,2:T(8,128)(2,1)} %copy-done.4) | copy-start | bytes 196612
  359.4 66.5 %copy-start.8 = (f32[4,256]{1,0:T(4,128)S(1)}, f32[4,256]{1,0:T(4,128)}, u32[]{:S(2)}) copy-start(f32[4,256]{1,0:T(4,128)} %copy-done.7) | copy-start | bytes 12292
  424.6 1.3 copy-start.6
  426.0 5.5 copy-start.3
  438.4 131.6 %reduce-scatter.9.cloned.1.call-start = ((), (), s32[]{:S(2)}) async-start(), calls=%async_computation.11 | async-start | bytes 557056 | tf_op jit(solution)/shard_map/reduce_scatter | solution.py:168
  439.7 216.8 %reduce-scatter.11.cloned.1.call-start = ((), (), s32[]{:S(2)}) async-start(), calls=%async_computation.12 | async-start | bytes 4456448 | tf_op jit(solution)/shard_map/reduce_scatter | solution.py:178
  509.6 146.9 %copy-start.2 = (bf16[256,512]{1,0:T(8,128)(2,1)S(1)}, bf16[256,512]{1,0:T(8,128)(2,1)}, u32[]{:S(2)}) copy-start(bf16[256,512]{1,0:T(8,128)(2,1)} %param.10) | copy-start | bytes 786436
Sparse Core Ops, SparseCore 0:
  52.2 53.6 all-gather.5
  108.7 54.4 all-gather.7
  174.6 42.5 all-gather.11
  219.5 43.5 all-gather.9
  279.7 79.2 reduce-scatter.4
  362.0 55.5 all-gather.13
  438.5 63.1 reduce-scatter.6
  505.4 64.5 reduce-scatter.8
  576.8 79.6 reduce-scatter.10
where the time goes:
time: 684 us
  waiting for transfers between devices  490 us (72%)
  matrix products  81.1 us (12%)
  blocking collectives  58.6 us (9%)
  local copies, waits for them, and re-layouts  21.9 us (3%)
  other arithmetic  16.8 us (2%)
  between operations  14.1 us (2%)
    reduce_scatter x1, waiting for transfers between devices, on_device(): lax.psum_scatter(partial_in.astype(jnp.bfloat16), 'tensor', scatter_dimen...  79.8 us
    reduce_scatter x1, waiting for transfers between devices, on_device(): lax.psum_scatter(partial_out.astype(jnp.bfloat16), 'tensor', scatter_dime...  79.4 us
    reduce_scatter x1, waiting for transfers between devices, on_device(): lax.psum_scatter(value_placed.astype(jnp.bfloat16), 'tensor', scatter_dim...  60.4 us
    all_gather x1, waiting for transfers between devices, on_device(): lax.all_gather(tangent_shard, 'tensor', axis=1, tiled=True)  58.2 us
    reduce_scatter x1, waiting for transfers between devices, on_device(): lax.psum_scatter(key_placed.astype(jnp.bfloat16), 'tensor', scatter_dimen...  52.9 us
    all_gather x1, waiting for transfers between devices, on_device(): lax.all_gather(tangent_part, 'tensor', axis=1, tiled=True)  52.8 us
    all_gather x1, waiting for transfers between devices, on_device(): lax.all_gather(clipped_part, 'tensor', axis=1, tiled=True)  50.3 us
    psum x1, blocking collectives, on_device(): square_total = lax.psum(jnp.sum(rows_float * rows_float, axis=1), 'tensor')  39.3 us
  transfers between devices with their start and end apart: 9, of which 9 were waited for; matrix products, arithmetic and copies ran while one was open for 8% of the time, Pallas kernels for 0%

commit v1 on v0

v1 whole, which is shorter than its diff:
```python
import functools
import math

import jax
import jax.numpy as jnp
from jax import lax
from jax.experimental import pallas as pl
from jax.experimental.pallas import tpu as pltpu
from jax.sharding import PartitionSpec as P

HEAD_DIM = 128
EPSILON = 1e-05
ROPE_BASE = 500000.0
MASKED = -1e30
MESH = pl.DeviceIdType.MESH
f32 = jnp.float32
bf16 = jnp.bfloat16

N_Y, N_Z, N_C = 2, 4, 2
N_T = N_Y * N_Z * N_C
TOK = 256
SHARD = 512
WIDTH = N_T * SHARD

RELS = [(dy, dz, dc) for dy in range(N_Y) for dz in range(N_Z) for dc in range(N_C)]
PEERS = [r for r in RELS if r != (0, 0, 0)]
CHIPS = [(0, 0), (0, 1), (0, 3), (1, 0), (0, 2), (1, 1), (1, 3), (1, 2)]


def ridx(rel):
    return (rel[0] * N_Z + rel[1]) * N_C + rel[2]


def peer(me, rel):
    y, z, c = me // (N_Z * N_C), (me // N_C) % N_Z, me % N_C
    y = (y + rel[0]) % N_Y
    z = (z + rel[1]) % N_Z
    c = (c + rel[2]) % N_C
    return (y * N_Z + z) * N_C + c


def source(me, rel):
    return peer(me, (-rel[0], -rel[1], -rel[2]))


def remote(src, dst, ssem, rsem, dp, target):
    return pltpu.make_async_remote_copy(
        src_ref=src, dst_ref=dst, send_sem=ssem, recv_sem=rsem, device_id=(dp, target), device_id_type=MESH
    )


def nt(a, b):
    return lax.dot_general(a, b, (((1,), (1,)), ((), ())), preferred_element_type=f32)


def tn(a, b):
    return lax.dot_general(a, b, (((0,), (0,)), ((), ())), preferred_element_type=f32)


def permutation():
    row = lax.broadcasted_iota(jnp.int32, (128, 128), 0)
    col = lax.broadcasted_iota(jnp.int32, (128, 128), 1)
    head, low = row // 16, row % 16
    want = jnp.where(low < 8, low * 8 + head, 64 + (low - 8) * 8 + head)
    return (col == want).astype(f32).astype(bf16)


def k1_body(
    x_ref, gain_ref, base_ref, pct_ref, step_ref, wq_hbm, wk_hbm, wv_hbm, cos_ref, sin_ref, cost_ref, sint_ref,
    qp_out, qt_out, kp_out, kt_out, vp_out, vt_out, rs_out, hid_out,
    hid, xs, wq, wkv, ss_send, ssr, rs, kvacc, qacc, kvt, kvr,
    wsem, hs, hr, fs, sss, ssrs, kvs, kvrs,
):
    me = lax.axis_index("tensor")
    dp = lax.axis_index("dp")
    barrier = pltpu.get_barrier_semaphore()
    for rel in PEERS:
        pl.semaphore_signal(barrier, inc=1, device_id=(dp, peer(me, rel)), device_id_type=MESH)
    loads = [
        pltpu.make_async_copy(wk_hbm, wkv.at[pl.ds(0, 64)], wsem.at[0]),
        pltpu.make_async_copy(wv_hbm, wkv.at[pl.ds(64, 64)], wsem.at[1]),
        pltpu.make_async_copy(wq_hbm, wq, wsem.at[2]),
    ]
    for load in loads:
        load.start()

    own = x_ref[...].astype(f32)
    square = own * own
    high = square.astype(bf16)
    low = (square - high.astype(f32)).astype(bf16)
    ones = jnp.ones((8, SHARD), bf16)
    ss_send[...] = nt(ones, high) + nt(ones, low)
    ssr[me] = ss_send[...]
    hid[me] = x_ref[...]

    pl.semaphore_wait(barrier, len(PEERS))
    sends = []
    for rel in PEERS:
        i = ridx(rel)
        cp = remote(ss_send, ssr.at[me], sss.at[i], ssrs.at[i], dp, peer(me, rel))
        cp.start()
        sends.append(cp)
    cp = remote(x_ref, hid.at[me], hs.at[1], hr.at[1], dp, peer(me, (0, 0, 1)))
    cp.start()
    sends.append(cp)
    for dy, dz in CHIPS[1:]:
        i = ridx((dy, dz, 0))
        cp = remote(x_ref, hid.at[me], hs.at[i], hr.at[i], dp, peer(me, (dy, dz, 0)))
        cp.start()
        sends.append(cp)
    for rel in PEERS:
        i = ridx(rel)
        remote(ss_send, ssr.at[source(me, rel)], sss.at[i], ssrs.at[i], dp, peer(me, rel)).wait_recv()
    total = jnp.sum(ssr[...], axis=0)
    scale = lax.rsqrt(total / WIDTH + EPSILON)
    rs[...] = jnp.transpose(jnp.broadcast_to(scale[0:1, :], (128, TOK)))
    rs_out[...] = rs[...]

    kvacc[...] = jnp.zeros_like(kvacc)

    def work(j):
        lanes = pl.ds(pl.multiple_of(j * SHARD, SHARD), SHARD)
        thresh = base_ref[:, lanes] * (1.0 + pct_ref[:, lanes].astype(f32) / 32.0)
        over = gain_ref[:, lanes] / thresh
        step = step_ref[:, lanes]

        def rows_step(r, carry):
            rows = pl.ds(pl.multiple_of(r * 32, 32), 32)
            rest = pl.ds(pl.multiple_of(TOK + r * 32, 32), 32)
            x = hid[j, rows, :].astype(f32)
            scale = rs[rows, :]
            for l in range(SHARD // 128):
                cut = slice(l * 128, l * 128 + 128)
                ratio = x[:, cut] * scale * over[:, cut]
                bent = jnp.tanh(ratio)
                xs[j, rows, cut] = (thresh[:, cut] * bent).astype(bf16)
                slope = bent - ratio * (1.0 - bent * bent)
                xs[j, rest, cut] = (slope * step[:, cut]).astype(bf16)
            return carry

        lax.fori_loop(0, TOK // 32, rows_step, 0)
        kvacc[...] += nt(xs[j], wkv[:, lanes])

    loads[0].wait()
    loads[1].wait()
    for dy, dz in CHIPS:
        if (dy, dz) != (0, 0):
            i = ridx((dy, dz, 0))
            j = source(me, (dy, dz, 0))
            remote(x_ref, hid.at[j], hs.at[i], hr.at[i], dp, me).wait_recv()
            i1 = ridx((dy, dz, 1))
            cp = remote(hid.at[j], hid.at[j], fs.at[i1], hr.at[i1], dp, peer(me, (0, 0, 1)))
            cp.start()
            sends.append(cp)
        work(source(me, (dy, dz, 0)))
        i1 = ridx((dy, dz, 1))
        j1 = source(me, (dy, dz, 1))
        remote(x_ref, hid.at[j1], hs.at[i1], hr.at[i1], dp, me).wait_recv()
        work(j1)

    kvt[...] = nt(permutation(), kvacc[...].astype(bf16)).astype(bf16)

    def block(chip):
        return pl.ds(pl.multiple_of(chip * 16, 16), 16)

    kvr[me] = kvt[block(me // N_C), :]
    for rel in PEERS:
        i = ridx(rel)
        to = peer(me, rel)
        cp = remote(kvt.at[block(to // N_C)], kvr.at[me], kvs.at[i], kvrs.at[i], dp, to)
        cp.start()
        sends.append(cp)

    loads[2].wait()
    qacc[...] = jnp.zeros_like(qacc)

    def q_step(j, carry):
        rows = pl.ds(pl.multiple_of(j * SHARD, SHARD), SHARD)
        qacc[...] += jnp.dot(xs[j], wq[rows, :], preferred_element_type=f32)
        return carry

    lax.fori_loop(0, N_T, q_step, 0)
    for h in range(4):
        cut = slice(h * 128, h * 128 + 128)
        for out, top in ((qp_out, 0), (qt_out, TOK)):
            z = qacc[pl.ds(top, TOK), cut]
            out[:, cut] = (z * cos_ref[...] + pltpu.roll(z, 64, 1) * sin_ref[...]).astype(bf16)

    for rel in PEERS:
        i = ridx(rel)
        remote(kvt.at[pl.ds(0, 16)], kvr.at[source(me, rel)], kvs.at[i], kvrs.at[i], dp, me).wait_recv()
    both = kvr[...].astype(f32)
    keys = both[:, 0:8, :].reshape(HEAD_DIM, 2 * TOK)
    vals = both[:, 8:16, :].reshape(HEAD_DIM, 2 * TOK).astype(bf16)
    vp_out[...] = vals[:, :TOK]
    vt_out[...] = vals[:, TOK:]
    cost, sint = cost_ref[...], sint_ref[...]
    for out, left in ((kp_out, 0), (kt_out, TOK)):
        z = keys[:, left : left + TOK]
        front, back = z[:64], z[64:]
        out[0:64, :] = (front * cost - back * sint).astype(bf16)
        out[64:128, :] = (back * cost + front * sint).astype(bf16)
    cp = pltpu.make_async_copy(hid, hid_out, wsem.at[0])
    cp.start()
    cp.wait()
    for cp in sends:
        cp.wait_send()


VM = pl.BlockSpec(memory_space=pltpu.VMEM)
ANY = pl.BlockSpec(memory_space=pl.ANY)


def k1(x, gain, base, pct, step, wq, wkt, wvt, cos, sin, cost, sint):
    sds = jax.ShapeDtypeStruct
    dma = pltpu.SemaphoreType.DMA((N_T,))
    return pl.pallas_call(
        k1_body,
        name="project",
        out_shape=[sds((TOK, SHARD), bf16)] * 2
        + [sds((HEAD_DIM, TOK), bf16)] * 4
        + [sds((TOK, 128), f32), sds((N_T, TOK, SHARD), bf16)],
        in_specs=[VM] * 5 + [ANY] * 3 + [VM] * 4,
        out_specs=[VM] * 7 + [ANY],
        scratch_shapes=[
            pltpu.VMEM((N_T, TOK, SHARD), bf16),
            pltpu.VMEM((N_T, 2 * TOK, SHARD), bf16),
            pltpu.VMEM((WIDTH, SHARD), bf16),
            pltpu.VMEM((128, WIDTH), bf16),
            pltpu.VMEM((8, TOK), f32),
            pltpu.VMEM((N_T, 8, TOK), f32),
            pltpu.VMEM((TOK, 128), f32),
            pltpu.VMEM((2 * TOK, 128), f32),
            pltpu.VMEM((2 * TOK, SHARD), f32),
            pltpu.VMEM((128, 2 * TOK), bf16),
            pltpu.VMEM((N_T, 16, 2 * TOK), bf16),
            pltpu.SemaphoreType.DMA((4,)),
            dma, dma, dma, dma, dma, dma, dma,
        ],
        compiler_params=pltpu.CompilerParams(collective_id=1, has_side_effects=True, vmem_limit_bytes=56 << 20),
    )(x, gain, base, pct, step, wq, wkt, wvt, cos, sin, cost, sint)


def contract_last(left_side, right_side):
    return nt(left_side, right_side)


def rotate(values, cosine, sine_part, turning):
    half_dim = values.shape[-1] // 2
    front_part = values[..., :half_dim]
    back_part = values[..., half_dim:]
    return jnp.concatenate(
        [
            front_part * cosine - turning * back_part * sine_part,
            back_part * cosine + turning * front_part * sine_part,
        ],
        axis=-1,
    )


def on_device(
    hidden_in, norm_gain, clip_base, pct_index, clip_step, w_query, w_key, w_value, w_out, doc_ids
):
    token_count = TOK
    me = lax.axis_index("tensor")
    score_scale = HEAD_DIM ** (-0.5)
    positions = jnp.arange(TOK, dtype=f32)
    frequency = jnp.exp(-math.log(ROPE_BASE) * 2.0 * jnp.arange(64, dtype=f32) / HEAD_DIM)
    angles = positions[:, None] * frequency[None, :]
    cosine, sine = jnp.cos(angles), jnp.sin(angles)
    cos2 = jnp.concatenate([cosine, cosine], axis=1)
    sin2 = jnp.concatenate([-sine, sine], axis=1)
    row = lambda v: v.reshape(1, WIDTH)
    query_p, query_t, kp, kt, vp, vt, rs, hid = k1(
        hidden_in, row(norm_gain), row(clip_base), row(pct_index), row(clip_step),
        w_query, w_key.T, w_value.T, cos2, sin2, cosine.T, sine.T,
    )
    query_p = query_p.reshape(TOK, 4, HEAD_DIM)
    query_t = query_t.reshape(TOK, 4, HEAD_DIM)
    key_p, key_t, value_p, value_t = kp.T, kt.T, vp.T, vt.T
    cosine, sine_part = cosine[:, None, :], sine[:, None, :]
    local_heads = 4
    doc_row = doc_ids[0]
    places = jnp.arange(token_count)
    allowed = (doc_row[:, None] == doc_row[None, :]) & (places[:, None] >= places[None, :])
    scores = jnp.einsum("shd,td->hst", query_p, key_p, preferred_element_type=f32) * score_scale
    attn_probs = jax.nn.softmax(jnp.where(allowed[None], scores, MASKED), axis=-1)
    probs_b = attn_probs.astype(bf16)
    tan_scores = (
        jnp.einsum("shd,td->hst", query_t, key_p, preferred_element_type=f32)
        + jnp.einsum("shd,td->hst", query_p, key_t, preferred_element_type=f32)
    ) * score_scale
    tan_probs = (
        attn_probs * (tan_scores - jnp.sum(attn_probs * tan_scores, axis=-1, keepdims=True))
    ).astype(bf16)
    tan_ctx = (
        jnp.einsum("hst,td->shd", tan_probs, value_p, preferred_element_type=f32)
        + jnp.einsum("hst,td->shd", probs_b, value_t, preferred_element_type=f32)
    ).astype(bf16)
    tan_ctx = tan_ctx.reshape(token_count, local_heads * HEAD_DIM)
    partial_out = jnp.dot(tan_ctx, w_out, preferred_element_type=f32)
    tangent_shard = (
        lax.psum_scatter(
            partial_out.astype(jnp.bfloat16), "tensor", scatter_dimension=1, tiled=True
        )
        .astype(jnp.float32)
        .astype(bf16)
    )
    back_ctx = contract_last(lax.all_gather(tangent_shard, "tensor", axis=1, tiled=True), w_out)
    back_ctx = back_ctx.astype(bf16).reshape(token_count, local_heads, HEAD_DIM)
    grad_prob = jnp.einsum("shd,td->hst", back_ctx, value_p, preferred_element_type=f32)
    grad_score = (
        attn_probs
        * (grad_prob - jnp.sum(attn_probs * grad_prob, axis=-1, keepdims=True))
        * score_scale
    ).astype(bf16)
    grad_query = (
        rotate(
            jnp.einsum("hst,td->shd", grad_score, key_p, preferred_element_type=f32),
            cosine,
            sine_part,
            -1.0,
        )
        .astype(bf16)
        .reshape(token_count, local_heads * HEAD_DIM)
    )
    key_local = jnp.sum(
        rotate(
            jnp.einsum("hst,shd->thd", grad_score, query_p, preferred_element_type=f32),
            cosine,
            sine_part,
            -1.0,
        ),
        axis=1,
    )
    value_local = jnp.einsum("hst,shd->td", probs_b, back_ctx, preferred_element_type=f32)
    key_heads, key_width, key_head = 8, 1024, me // 2
    selector = (jnp.arange(key_heads) == key_head).astype(f32)
    key_placed = (key_local.astype(bf16).astype(f32)[:, :, None] * selector).reshape(
        token_count, key_width
    )
    value_placed = (value_local.astype(bf16).astype(f32)[:, :, None] * selector).reshape(
        token_count, key_width
    )
    grad_key, grad_value = (
        lax.psum_scatter(
            key_placed.astype(jnp.bfloat16), "tensor", scatter_dimension=1, tiled=True
        ).astype(jnp.float32),
        lax.psum_scatter(
            value_placed.astype(jnp.bfloat16), "tensor", scatter_dimension=1, tiled=True
        ).astype(jnp.float32),
    )
    partial_in = (
        contract_last(grad_query, w_query)
        + contract_last(grad_key.astype(bf16), w_key)
        + contract_last(grad_value.astype(bf16), w_value)
    )
    thresh = clip_base * (1.0 + pct_index.astype(f32) / 32.0)
    hidden = jnp.transpose(hid, (1, 0, 2)).reshape(TOK, WIDTH).astype(f32)
    ratios = hidden * rs[:, 0:1] * norm_gain / thresh
    bent = jnp.tanh(ratios)
    slopes = bent - ratios * (1.0 - bent * bent)
    token_total = token_count * lax.axis_size("dp")
    channel = jnp.sum(partial_in * slopes, axis=0) / token_total
    channel = lax.psum_scatter(channel, "tensor", scatter_dimension=0, tiled=True)
    gn_product = lax.psum(channel, "dp")
    return (tangent_shard, gn_product)


def solution(mesh):
    in_specs = (
        P("dp", "tensor"),
        P(),
        P(),
        P(),
        P(),
        P(None, "tensor"),
        P(None, "tensor"),
        P(None, "tensor"),
        P("tensor", None),
        P("dp", None),
    )
    out_specs = (P("dp", "tensor"), P("tensor"))
    return jax.shard_map(
        on_device, mesh=mesh, in_specs=in_specs, out_specs=out_specs, check_vma=False
    )
```

time: 684 us -> 460 us (0.67)
  waiting for transfers between devices: 490 us -> 227 us
  Pallas kernels: 0 us -> 48.4 us
  matrix products: 81.1 us -> 52.9 us
  blocking collectives: 58.6 us -> 84.8 us
    all_gather x4 -> x0, waiting for transfers between devices: 159 us -> none  [the longest x1 52.8 us: on_device(): lax.all_gather(tangent_part, 'tensor', axis=1, tiled=True)]
    reduce_scatter x1 -> x0, waiting for transfers between devices: 79.8 us -> none  [on_device(): lax.psum_scatter(partial_in.astype(jnp.bfloat16), 'tensor', scatter_dimen...]
    unnamed x0 -> x1, blocking collectives: none -> 65.1 us
    pallas_call x0 -> x1, Pallas kernels: none -> 48.4 us  [k1(): pl.pallas_call(k1_body, name='project', out_shape=[sds((TOK, SHARD), bf16...]
    psum x1 -> x0, blocking collectives: 39.3 us -> none  [on_device(): square_total = lax.psum(jnp.sum(rows_float * rows_float, axis=1), 'tensor')]
    reduce_scatter x1, waiting for transfers between devices: 52.9 us -> 27.8 us  [on_device(): lax.psum_scatter(key_placed.astype(jnp.bfloat16), 'tensor', scatter_dimen...]
    dot_general x7 -> x4, matrix products: 53.4 us -> 31.7 us  [nt(): lax.dot_general(a, b, (((1,), (1,)), ((), ())), preferred_element_type=f32)]
    convert_element_type x1 -> x2, local copies, waits for them, and re-layouts: 0.11 us -> 18.3 us  [on_device(): hidden = jnp.transpose(hid, (1, 0, 2)).reshape(TOK, WIDTH).astype(f32)]
  transfers between devices with their start and end apart: 9 -> 4, of which waited for: 9 -> 4; matrix products, arithmetic and copies ran while one was open for 8% -> 9% of each run, Pallas kernels for 0% -> 0%
where the time goes in v1:
time: 460 us; the launch traced here: 459 us
  waiting for transfers between devices  227 us (49%)
  blocking collectives  84.8 us (18%)
  matrix products  52.9 us (12%)
  Pallas kernels  48.4 us (11%)
  local copies, waits for them, and re-layouts  19.5 us (4%)
  between operations  14.7 us (3%)
  other arithmetic  11.1 us (2%)
    reduce_scatter x1, waiting for transfers between devices, on_device(): lax.psum_scatter(partial_out.astype(jnp.bfloat16), 'tensor', scatter_dime...  81.1 us
    unnamed x1, blocking collectives  65.1 us
    reduce_scatter x1, waiting for transfers between devices, on_device(): lax.psum_scatter(value_placed.astype(jnp.bfloat16), 'tensor', scatter_dim...  60.3 us
    all_gather x1, waiting for transfers between devices, on_device(): lax.all_gather(tangent_shard, 'tensor', axis=1, tiled=True)  58.1 us
    pallas_call x1, Pallas kernels, k1(): pl.pallas_call(k1_body, name='project', out_shape=[sds((TOK, SHARD), bf16...  48.4 us
    dot_general x4, matrix products, nt(): lax.dot_general(a, b, (((1,), (1,)), ((), ())), preferred_element_type=f32)  31.7 us
    reduce_scatter x1, waiting for transfers between devices, on_device(): lax.psum_scatter(key_placed.astype(jnp.bfloat16), 'tensor', scatter_dimen...  27.8 us
    psum x1, blocking collectives, on_device(): gn_product = lax.psum(channel, 'dp')  19.8 us
  transfers between devices with their start and end apart: 4, of which 4 were waited for; matrix products, arithmetic and copies ran while one was open for 9% of the time, Pallas kernels for 0%

profile of v1, /device:TPU:0, one launch (start us, length us, event | category | flops | bytes accessed | tf_op | source)
XLA Modules:
  0.0 459.2 jit_solution(10240685620250890041)
XLA Ops:
  7.2 0.0 reduce-scatter.4.cloned.1.call-start
  7.2 0.5 fusion.46
  7.7 1.0 fusion.64
  8.7 0.9 fusion.38
  9.6 0.8 pad_maximum_fusion.1
  10.4 48.4 %project.1 = (bf16[256,512]{1,0:T(8,128)(2,1)}, bf16[256,512]{1,0:T(8,128)(2,1)}, bf16[128,256]{1,0:T(8,128)(2,1)}, bf16[128,256]{1,0:T(8,128)(2,1)}, bf16[128,2...) custom-call(bf16[256,512]{1,0:T(8,128)(2,1)} %x_ref.1, ...), custom_call_target="tpu_custom_call" | custom-call | tf_op jit(solution)/shard_map/project/pallas_call | solution.py:217
  58.8 0.0 copy-start.5
  58.8 0.0 copy-start.8
  58.9 1.4 fusion.30
  60.2 1.5 fusion.96
  61.7 2.6 multiply_reduce_fusion
  64.3 2.2 fusion.24
  66.6 0.7 fusion.14
  67.3 7.7 %convolution_convert_fusion = bf16[256,8192]{1,0:T(8,128)(2,1)} fusion(bf16[256,512]{0,1:T(8,128)(2,1)S(1)} %bitcast.182, bf16[512,8192]{1,0:T(8,128)(2,1)} %param.18), kind=kOutput, calls=%fused_computation.5 | convolution fusion | flops 2149580800 | bytes 12845056 | tf_op jit(solution)/shard_map/dot_general | solution.py:301
  75.0 0.0 reduce-scatter.4.cloned.1.call-update
  75.0 0.0 all-gather.2.cloned.1.call-start
  75.1 81.1 %reduce-scatter.4.cloned.1.call-done = bf16[256,512]{1,0:T(8,128)(2,1)} async-done(((bf16[256,8192]{1,0:T(8,128)(2,1)}), bf16[256,512]{1,0:T(8,128)(2,1)}) %reduce-scatter.4.cloned.1.call-update) | async-done | bytes 262160 | tf_op jit(solution)/shard_map/reduce_scatter | solution.py:303
  156.2 0.0 all-gather.2.cloned.1.call-update
  156.2 0.2 reduce-scatter.6.cloned.1.call-start
  156.4 0.1 copy.78
  156.5 0.1 copy.79
  156.6 0.1 mul.302
  156.7 58.1 %all-gather.2.cloned.1.call-done = bf16[256,8192]{1,0:T(8,128)(2,1)} async-done(((bf16[256,512]{1,0:T(8,128)(2,1)}), bf16[256,8192]{1,0:T(8,128)(2,1)}) %all-gather.2.cloned.1.call-update) | async-done | bytes 4194320 | tf_op jit(solution)/shard_map/all_gather | solution.py:309
  214.9 7.0 %fusion.15 = bf16[32,4,8,128]{3,2,1,0:T(8,128)(2,1)S(1)} fusion(bf16[256,8192]{1,0:T(8,128)(2,1)} %all-gather.2.cloned.1.call-done, bf16[512,8192]{1,0:T(8,128)(2,1)} %param.18), kind=kOutput, calls=%fused_computation.26 | convolution fusion | flops 2147614720 | bytes 12845056 | tf_op jit(solution)/shard_map/dot_general | solution.py:53
  221.9 0.3 convolution_bitcast_fusion
  222.2 2.0 convolution_bitcast_fusion.1
  224.3 2.0 convolution_bitcast_fusion.2
  226.3 0.8 fusion.17
  227.1 0.1 copy.83
  227.2 0.1 multiply_subtract_fusion
  227.4 1.2 fusion.18
  228.6 0.0 reduce-scatter.6.cloned.1.call-update
  228.6 0.0 reduce-scatter.8.cloned.1.call-start
  228.6 6.6 %convert_bitcast_fusion = f32[256,16,512]{2,0,1:T(8,128)} fusion(bf16[16,256,512]{2,1,0:T(8,128)(2,1)} %get-tuple-element.16), kind=kLoop, calls=%fused_computation.6 | loop fusion | flops 2097152 | bytes 12582912 | tf_op jit(solution)/shard_map/convert_element_type | solution.py:359
  235.2 9.3 %copy.84 = f32[256,16,512]{0,2,1:T(8,128)} copy(f32[256,16,512]{2,0,1:T(8,128)} %convert_bitcast_fusion) | data formatting | bytes 16777216 | tf_op jit(solution)/shard_map/convert_element_type | solution.py:359
  244.5 9.0 %copy.85 = f32[256,8192]{1,0:T(8,128)} copy(f32[256,8192]{0,1:T(8,128)} %bitcast.178) | data formatting | bytes 16777216 | tf_op jit(solution)/shard_map/convert_element_type | solution.py:359
  253.6 0.6 dynamic-slice
  254.8 0.1 slice_reduce_fusion
  255.0 0.0 reduce-scatter.8.cloned.1.call-update
  255.0 0.0 copy-start
  255.0 9.1 %fusion.101 = f32[256,8192]{1,0:T(8,128)} fusion(bf16[256,512]{0,1:T(8,128)(2,1)S(1)} %bitcast.180, bf16[8192,512]{1,0:T(8,128)(2,1)} %wq_hbm.1), kind=kOutput, calls=%fused_computation.99 | convolution fusion | flops 2147483648 | bytes 17039360 | tf_op jit(solution)/shard_map/dot_general | solution.py:53
  264.1 27.8 %reduce-scatter.6.cloned.1.call-done = bf16[256,64]{0,1:T(8,128)(2,1)} async-done(((bf16[256,1024]{0,1:T(8,128)(2,1)}), bf16[256,64]{0,1:T(8,128)(2,1)}) %reduce-scatter.6.cloned.1.call-update) | async-done | bytes 32784 | tf_op jit(solution)/shard_map/reduce_scatter | solution.py:346
  291.9 7.9 %convolution_add_fusion.1 = f32[256,8192]{1,0:T(8,128)} fusion(f32[256,8192]{1,0:T(8,128)} %fusion.101, bf16[256,64]{0,1:T(8,128)(2,1)} %reduce-scatter.6.cloned.1.call-done, bf16[8192,64]{0,1:T(8,128)(2,1)S(1)} %copy-done), kind=kOutput, calls=%fused_computation.4 | convolution fusion | flops 270532608 | bytes 17858560 | tf_op jit(solution)/shard_map/dot_general | solution.py:53
  299.8 60.3 %reduce-scatter.8.cloned.1.call-done = bf16[256,64]{0,1:T(8,128)(2,1)} async-done(((bf16[256,1024]{0,1:T(8,128)(2,1)}), bf16[256,64]{0,1:T(8,128)(2,1)}) %reduce-scatter.8.cloned.1.call-update) | async-done | bytes 32784 | tf_op jit(solution)/shard_map/reduce_scatter | solution.py:349
  360.1 7.6 %fusion.3 = f32[8192]{0:T(1024)S(1)} fusion(f32[8192]{0:T(1024)S(1)} %add_multiply_fusion, f32[8192]{0:T(1024)S(1)} %copy-done.7, f32[256,8192]{1,0:T(8,128)} %copy.85, f32[256]{0:T(256)S(1)} %slice_reduce_fusion, f32[256,8192]{1,0:T(8,128)} %convolution_add_fusion.1, bf16[256,64]{0,1:T(8,128)(2,1)} %reduce-scatter.8.cloned.1.call-done, ...), kind=kOutput, calls=%fused_computation.7 | convolution fusion | flops 289398784 | bytes 17957888 | tf_op jit(solution)/shard_map/dot_general | solution.py:53
  367.7 65.1 %all-reduce = f32[8192]{0:T(1024)S(1)} all-reduce(f32[8192]{0:T(1024)S(1)} %broadcast_multiply_fusion), channel_id=5, replica_groups=mesh['dp'=8,'tensor'=16] {'tensor'}, use_global_device_ids=true, to_apply=%region_9.10.clone | all-reduce | flops 8192 | bytes 65536
  432.8 0.1 dynamic-slice.1
  432.9 19.8 %psum.7 = f32[512]{0:T(512)} all-reduce(f32[512]{0:T(512)S(1)} %dynamic-slice.1), channel_id=1, replica_groups=mesh['dp'=8,'tensor'=16] {'dp'}, use_global_device_ids=true, to_apply=%region_10.11 | all-reduce | flops 512 | bytes 4096 | tf_op jit(solution)/shard_map/psum | solution.py:366
  (29 shorter events, 0.1 us)
Async XLA Ops:
  7.2 149.0 %reduce-scatter.4.cloned.1.call-start = ((), (), s32[]{:S(2)}) async-start(), calls=%async_computation.3 | async-start | bytes 4456448 | tf_op jit(solution)/shard_map/reduce_scatter | solution.py:303
  58.8 7.7 %copy-start.5 = (bf16[128,256]{1,0:T(8,128)(2,1)S(1)}, bf16[128,256]{1,0:T(8,128)(2,1)}, u32[]{:S(2)}) copy-start(bf16[128,256]{1,0:T(8,128)(2,1)} %get-tuple-element.11) | copy-start | bytes 196612
  58.8 7.7 %copy-start.8 = (bf16[256,512]{1,0:T(8,128)(2,1)S(1)}, bf16[256,512]{1,0:T(8,128)(2,1)}, u32[]{:S(2)}) copy-start(bf16[256,512]{1,0:T(8,128)(2,1)} %get-tuple-element.12) | copy-start | bytes 786436
  58.8 7.7 %copy-start.9 = (bf16[128,256]{1,0:T(8,128)(2,1)S(1)}, bf16[128,256]{1,0:T(8,128)(2,1)}, u32[]{:S(2)}) copy-start(bf16[128,256]{1,0:T(8,128)(2,1)} %get-tuple-element.15) | copy-start | bytes 196612
  61.7 13.3 %copy-start.11 = (f32[4,256,256]{1,2,0:T(8,128)}, f32[4,256,256]{1,2,0:T(8,128)S(1)}, u32[]{:S(2)}) copy-start(f32[4,256,256]{1,2,0:T(8,128)S(1)} %get-tuple-element.33) | copy-start | bytes 3145732
  75.0 146.9 %copy-start.6 = (bf16[128,256]{1,0:T(8,128)(2,1)S(1)}, bf16[128,256]{1,0:T(8,128)(2,1)}, u32[]{:S(2)}) copy-start(bf16[128,256]{1,0:T(8,128)(2,1)} %get-tuple-element.10) | copy-start | bytes 196612
  75.0 139.9 %all-gather.2.cloned.1.call-start = ((), (), s32[]{:S(2)}) async-start(), calls=%async_computation.4 | async-start | bytes 4456448 | tf_op jit(solution)/shard_map/all_gather | solution.py:309
  156.2 135.7 %reduce-scatter.6.cloned.1.call-start = ((), (), s32[]{:S(2)}) async-start(), calls=%async_computation.5 | async-start | bytes 557056 | tf_op jit(solution)/shard_map/reduce_scatter | solution.py:346
  228.6 131.4 %reduce-scatter.8.cloned.1.call-start = ((), (), s32[]{:S(2)}) async-start(), calls=%async_computation.6 | async-start | bytes 557056 | tf_op jit(solution)/shard_map/reduce_scatter | solution.py:349
  244.5 9.0 %copy-start.10 = (u32[128]{0:T(128)S(1)}, u32[128]{0:T(128)}, u32[]{:S(2)}) copy-start(u32[128]{0:T(128)} %constant.46) | copy-start | bytes 1540
  244.5 10.3 %copy-start.4 = (f32[256,128]{1,0:T(8,128)S(1)}, f32[256,128]{1,0:T(8,128)}, u32[]{:S(2)}) copy-start(f32[256,128]{1,0:T(8,128)} %get-tuple-element.17) | copy-start | bytes 393220
  244.5 10.4 %copy-start.2 = (f32[8192]{0:T(1024)S(1)}, f32[8192]{0:T(1024)}, u32[]{:S(2)}) copy-start(f32[8192]{0:T(1024)} %param.12) | copy-start | bytes 98308
  244.5 10.4 %copy-start.3 = (s32[8192]{0:T(1024)S(1)}, s32[8192]{0:T(1024)}, u32[]{:S(2)}) copy-start(s32[8192]{0:T(1024)} %param.13) | copy-start | bytes 98308
  255.0 36.9 %copy-start = (bf16[8192,64]{0,1:T(8,128)(2,1)S(1)}, bf16[8192,64]{0,1:T(8,128)(2,1)}, u32[]{:S(2)}) copy-start(bf16[8192,64]{0,1:T(8,128)(2,1)} %param.16) | copy-start | bytes 3145732
  264.1 95.9 %copy-start.1 = (bf16[8192,64]{0,1:T(8,128)(2,1)S(1)}, bf16[8192,64]{0,1:T(8,128)(2,1)}, u32[]{:S(2)}) copy-start(bf16[8192,64]{0,1:T(8,128)(2,1)} %param.17) | copy-start | bytes 3145732
  264.1 95.9 %copy-start.7 = (f32[8192]{0:T(1024)S(1)}, f32[8192]{0:T(1024)}, u32[]{:S(2)}) copy-start(f32[8192]{0:T(1024)} %param.11) | copy-start | bytes 98308
Sparse Core Ops, SparseCore 0:
  75.1 80.9 reduce-scatter.3
  159.3 55.5 all-gather.1
  228.7 63.1 reduce-scatter.5
  295.5 64.5 reduce-scatter.7

commit v2 on v1

v2 whole, which is shorter than its diff:
```python
import functools
import math

import jax
import jax.numpy as jnp
import numpy as np
from jax import lax
from jax.experimental import pallas as pl
from jax.experimental.pallas import tpu as pltpu
from jax.sharding import PartitionSpec as P

HEAD_DIM = 128
EPSILON = 1e-05
ROPE_BASE = 500000.0
MASKED = -1e30
MESH = pl.DeviceIdType.MESH
f32 = jnp.float32
bf16 = jnp.bfloat16

N_Y, N_Z, N_C = 2, 4, 2
N_T = N_Y * N_Z * N_C
TOK = 256
SHARD = 512
WIDTH = N_T * SHARD
HEADS = 4
N_DP = 8
VMEM_BYTES = 60 << 20

RELS = [(dy, dz, dc) for dy in range(N_Y) for dz in range(N_Z) for dc in range(N_C)]
PEERS = [r for r in RELS if r != (0, 0, 0)]
CHIPS = [(0, 0), (0, 1), (0, 3), (1, 0), (0, 2), (1, 1), (1, 3), (1, 2)]


def ridx(rel):
    return (rel[0] * N_Z + rel[1]) * N_C + rel[2]


def peer(me, rel):
    y, z, c = me // (N_Z * N_C), (me // N_C) % N_Z, me % N_C
    y = (y + rel[0]) % N_Y
    z = (z + rel[1]) % N_Z
    c = (c + rel[2]) % N_C
    return (y * N_Z + z) * N_C + c


def source(me, rel):
    return peer(me, (-rel[0], -rel[1], -rel[2]))


def remote(src, dst, ssem, rsem, dp, target):
    return pltpu.make_async_remote_copy(
        src_ref=src, dst_ref=dst, send_sem=ssem, recv_sem=rsem, device_id=(dp, target), device_id_type=MESH
    )


def nt(a, b):
    return lax.dot_general(a, b, (((1,), (1,)), ((), ())), preferred_element_type=f32)


def tn(a, b):
    return lax.dot_general(a, b, (((0,), (0,)), ((), ())), preferred_element_type=f32)


def permutation():
    row = lax.broadcasted_iota(jnp.int32, (128, 128), 0)
    col = lax.broadcasted_iota(jnp.int32, (128, 128), 1)
    head, low = row // 16, row % 16
    want = jnp.where(low < 8, low * 8 + head, 64 + (low - 8) * 8 + head)
    return (col == want).astype(f32).astype(bf16)


def body(
    x_ref, gain_ref, base_ref, pct_ref, step_ref, doc_ref, cos_ref, sin_ref, cost_ref, sint_ref,
    wq_hbm, wk_hbm, wv_hbm, wo_hbm,
    out_ref, gn_ref,
    hid, xs, slopes, wq, wkv, wo, ss_send, ssr, rs, kvacc, qacc, kvt, kvr, qp, qt, kp, kt, vp, vt, docs, probs, ctx,
    pair_out, pair_in, part_out, part_in, tg, bacc, gq, gkv_out, gkv_in, gkv, gnv, gnv_in, dpv, dpv_in,
    wsem, hs, hr, fs, sss, ssrs, kvs, kvrs, ps, pr, qs, qr, gs, gr, gf, ks, kr, ns, nr, ds, dr,
):
    me = lax.axis_index("tensor")
    dp = lax.axis_index("dp")
    sibling = peer(me, (0, 0, 1))
    barrier = pltpu.get_barrier_semaphore()
    for rel in PEERS:
        pl.semaphore_signal(barrier, inc=1, device_id=(dp, peer(me, rel)), device_id_type=MESH)
    for d in range(1, N_DP):
        pl.semaphore_signal(barrier, inc=1, device_id=((dp + d) % N_DP, me), device_id_type=MESH)
    loads = [
        pltpu.make_async_copy(wk_hbm, wkv.at[pl.ds(0, 64)], wsem.at[0]),
        pltpu.make_async_copy(wv_hbm, wkv.at[pl.ds(64, 64)], wsem.at[1]),
        pltpu.make_async_copy(wq_hbm, wq, wsem.at[2]),
        pltpu.make_async_copy(wo_hbm, wo, wsem.at[3]),
    ]
    for load in loads:
        load.start()

    sends = []

    def send(src, dst, ssem, rsem, to, group=None):
        cp = remote(src, dst, ssem, rsem, dp if group is None else group, to)
        cp.start()
        sends.append(cp)

    def arrived(dst, ssem, rsem):
        remote(dst, dst, ssem, rsem, dp, me).wait_recv()

    own = x_ref[...].astype(f32)
    square = own * own
    high = square.astype(bf16)
    low = (square - high.astype(f32)).astype(bf16)
    ones = jnp.ones((8, SHARD), bf16)
    ss_send[...] = nt(ones, high) + nt(ones, low)
    ssr[me] = ss_send[...]
    hid[me] = x_ref[...]
    docs[...] = jnp.transpose(jnp.broadcast_to(doc_ref[...].astype(f32), (128, TOK)))

    pl.semaphore_wait(barrier, len(PEERS) + N_DP - 1)
    for rel in PEERS:
        i = ridx(rel)
        send(ss_send, ssr.at[me], sss.at[i], ssrs.at[i], peer(me, rel))
    send(x_ref, hid.at[me], hs.at[1], hr.at[1], sibling)
    for dy, dz in CHIPS[1:]:
        i = ridx((dy, dz, 0))
        send(x_ref, hid.at[me], hs.at[i], hr.at[i], peer(me, (dy, dz, 0)))
    for rel in PEERS:
        i = ridx(rel)
        arrived(ssr.at[source(me, rel)], sss.at[i], ssrs.at[i])
    total = jnp.sum(ssr[...], axis=0)
    scale = lax.rsqrt(total / WIDTH + EPSILON)
    rs[...] = jnp.transpose(jnp.broadcast_to(scale[0:1, :], (128, TOK)))

    kvacc[...] = jnp.zeros_like(kvacc)

    def lanes_of(j):
        return pl.ds(pl.multiple_of(j * SHARD, SHARD), SHARD)

    def work(j):
        lanes = lanes_of(j)
        thresh = base_ref[:, lanes] * (1.0 + pct_ref[:, lanes].astype(f32) / 32.0)
        over = gain_ref[:, lanes] / thresh
        step = step_ref[:, lanes]

        def rows_step(r, carry):
            rows = pl.ds(pl.multiple_of(r * 32, 32), 32)
            rest = pl.ds(pl.multiple_of(TOK + r * 32, 32), 32)
            x = hid[j, rows, :].astype(f32)
            scale = rs[rows, :]
            for l in range(SHARD // 128):
                cut = slice(l * 128, l * 128 + 128)
                ratio = x[:, cut] * scale * over[:, cut]
                bent = jnp.tanh(ratio)
                xs[j, rows, cut] = (thresh[:, cut] * bent).astype(bf16)
                slope = bent - ratio * (1.0 - bent * bent)
                slopes[j, rows, cut] = slope
                xs[j, rest, cut] = (slope * step[:, cut]).astype(bf16)
            return carry

        lax.fori_loop(0, TOK // 32, rows_step, 0)
        kvacc[...] += nt(xs[j], wkv[:, lanes])

    loads[0].wait()
    loads[1].wait()

    def gather(buf, ssem, rsem, fsem, use):
        for dy, dz in CHIPS:
            j = source(me, (dy, dz, 0))
            i1 = ridx((dy, dz, 1))
            if (dy, dz) != (0, 0):
                i = ridx((dy, dz, 0))
                arrived(buf.at[j], ssem.at[i], rsem.at[i])
                send(buf.at[j], buf.at[j], fsem.at[i1], rsem.at[i1], sibling)
            use(j)
            j1 = source(me, (dy, dz, 1))
            arrived(buf.at[j1], ssem.at[i1], rsem.at[i1])
            use(j1)

    gather(hid, hs, hr, fs, work)

    kvt[...] = nt(permutation(), kvacc[...].astype(bf16)).astype(bf16)

    def block(chip):
        return pl.ds(pl.multiple_of(chip * 16, 16), 16)

    kvr[me] = kvt[block(me // N_C), :]
    for rel in PEERS:
        i = ridx(rel)
        to = peer(me, rel)
        send(kvt.at[block(to // N_C)], kvr.at[me], kvs.at[i], kvrs.at[i], to)

    loads[2].wait()
    qacc[...] = jnp.zeros_like(qacc)

    def q_step(j, carry):
        qacc[...] += jnp.dot(xs[j], wq[lanes_of(j), :], preferred_element_type=f32)
        return carry

    lax.fori_loop(0, N_T, q_step, 0)
    for h in range(HEADS):
        cut = slice(h * 128, h * 128 + 128)
        for out, top in ((qp, 0), (qt, TOK)):
            z = qacc[pl.ds(top, TOK), cut]
            out[:, cut] = (z * cos_ref[...] + pltpu.roll(z, 64, 1) * sin_ref[...]).astype(bf16)

    for rel in PEERS:
        i = ridx(rel)
        arrived(kvr.at[source(me, rel)], kvs.at[i], kvrs.at[i])
    both = kvr[...].astype(f32)
    keys = both[:, 0:8, :].reshape(HEAD_DIM, 2 * TOK)
    vals = both[:, 8:16, :].reshape(HEAD_DIM, 2 * TOK).astype(bf16)
    vp[...] = vals[:, :TOK]
    vt[...] = vals[:, TOK:]
    cost, sint = cost_ref[...], sint_ref[...]
    for out, left in ((kp, 0), (kt, TOK)):
        z = keys[:, left : left + TOK]
        front, back = z[:64], z[64:]
        out[0:64, :] = (front * cost - back * sint).astype(bf16)
        out[64:128, :] = (back * cost + front * sint).astype(bf16)

    same = jnp.concatenate([docs[...], docs[...]], axis=1) == doc_ref[...].astype(f32)
    place = lax.broadcasted_iota(jnp.int32, (TOK, TOK), 0) >= lax.broadcasted_iota(jnp.int32, (TOK, TOK), 1)
    allowed = same & place
    score_scale = HEAD_DIM ** (-0.5)

    def dot(a, b):
        return jnp.dot(a, b, preferred_element_type=f32)

    for h in range(HEADS):
        cut = slice(h * 128, h * 128 + 128)
        q0, q1 = qp[:, cut], qt[:, cut]
        scores = jnp.where(allowed, dot(q0, kp[...]) * score_scale, MASKED)
        grown = jnp.exp(scores - jnp.max(scores, axis=1, keepdims=True))
        prob = grown / jnp.sum(grown, axis=1, keepdims=True)
        probs[h] = prob
        t = (dot(q1, kp[...]) + dot(q0, kt[...])) * score_scale
        tan = (prob * (t - jnp.sum(prob * t, axis=1, keepdims=True))).astype(bf16)
        ctx[:, cut] = (nt(tan, vp[...]) + nt(prob.astype(bf16), vt[...])).astype(bf16)

    loads[3].wait()
    order = CHIPS[::-1]

    def pair_part(s):
        dy, dz = order[s]
        pair_out[s] = dot(ctx[...], wo[:, lanes_of(peer(me, (dy, dz, 1)))]).astype(bf16)
        send(pair_out.at[s], pair_in.at[s], ps.at[s], pr.at[s], sibling)

    def own_part(s):
        dy, dz = order[s]
        to = peer(me, (dy, dz, 0))
        mine = dot(ctx[...], wo[:, lanes_of(to)]).astype(bf16).astype(f32)
        arrived(pair_in.at[s], ps.at[s], pr.at[s])
        part_out[s] = (mine + pair_in[s].astype(f32)).astype(bf16)
        if s < 7:
            send(part_out.at[s], part_in.at[s], qs.at[s], qr.at[s], to)

    pair_part(0)
    pair_part(1)
    for s in range(8):
        if s + 2 < 8:
            pair_part(s + 2)
        own_part(s)
    for s in range(7):
        arrived(part_in.at[s], qs.at[s], qr.at[s])

    def sum_step(r, carry):
        rows = pl.ds(pl.multiple_of(r * 32, 32), 32)
        value = part_out[7, rows, :].astype(f32)
        for s in range(7):
            value = value + part_in[s, rows, :].astype(f32)
        tg[me, rows, :] = value.astype(bf16)
        return carry

    lax.fori_loop(0, TOK // 32, sum_step, 0)
    send(tg.at[me], tg.at[me], gs.at[1], gr.at[1], sibling)
    for dy, dz in CHIPS[1:]:
        i = ridx((dy, dz, 0))
        send(tg.at[me], tg.at[me], gs.at[i], gr.at[i], peer(me, (dy, dz, 0)))
    out_ref[...] = tg[me]
    bacc[...] = jnp.zeros_like(bacc)

    def back(j):
        bacc[...] += nt(tg[j], wo[:, lanes_of(j)])

    gather(tg, gs, gr, gf, back)

    gk = jnp.zeros((HEAD_DIM, TOK), f32)
    gv = jnp.zeros((HEAD_DIM, TOK), f32)
    for h in range(HEADS):
        cut = slice(h * 128, h * 128 + 128)
        bc = bacc[:, cut].astype(bf16)
        prob = probs[h]
        g = dot(bc, vp[...])
        score = (prob * (g - jnp.sum(prob * g, axis=1, keepdims=True)) * score_scale).astype(bf16)
        z = nt(score, kp[...])
        gq[:, cut] = (z * cos_ref[...] - pltpu.roll(z, 64, 1) * sin_ref[...]).astype(bf16)
        gk = gk + tn(qp[:, cut], score)
        gv = gv + tn(bc, prob.astype(bf16))
    front, back_half = gk[:64], gk[64:]
    gk = jnp.concatenate([front * cost + back_half * sint, back_half * cost - front * sint], axis=0)
    gkv_out[...] = jnp.concatenate([gk.reshape(N_T, 8, TOK), gv.reshape(N_T, 8, TOK)], axis=1).astype(bf16)
    gkv_in[me] = gkv_out[me]
    for rel in PEERS:
        i = ridx(rel)
        to = peer(me, rel)
        send(gkv_out.at[to], gkv_in.at[me], ks.at[i], kr.at[i], to)

    def column_sums(product):
        line = jnp.sum(product, axis=0, keepdims=True)
        return jnp.concatenate([line[:, l * 128 : l * 128 + 128] for l in range(4)] * 2, axis=0)

    def query_step(j, carry):
        gnv[j] = column_sums(nt(gq[...], wq[lanes_of(j), :]) * slopes[j])
        return carry

    lax.fori_loop(0, N_T, query_step, 0)
    for rel in PEERS:
        i = ridx(rel)
        arrived(gkv_in.at[source(me, rel)], ks.at[i], kr.at[i])
    pairs = gkv_in[...].astype(f32).reshape(N_T // 2, 2, 16, TOK)
    summed = (pairs[:, 0] + pairs[:, 1]).reshape(HEAD_DIM, TOK).astype(bf16)
    gkv[...] = tn(summed, permutation()).astype(bf16)

    def key_step(j, carry):
        gnv[j] += column_sums(dot(gkv[...], wkv[:, lanes_of(j)]) * slopes[j])
        return carry

    lax.fori_loop(0, N_T, key_step, 0)
    gnv_in[me] = gnv[me]
    for rel in PEERS:
        i = ridx(rel)
        to = peer(me, rel)
        send(gnv.at[to], gnv_in.at[me], ns.at[i], nr.at[i], to)
    for rel in PEERS:
        i = ridx(rel)
        arrived(gnv_in.at[source(me, rel)], ns.at[i], nr.at[i])
    dpv[...] = jnp.sum(gnv_in[...], axis=0)
    dpv_in[dp] = dpv[...]
    for d in range(1, N_DP):
        send(dpv, dpv_in.at[dp], ds.at[d], dr.at[d], me, (dp + d) % N_DP)
    for d in range(1, N_DP):
        arrived(dpv_in.at[(dp + N_DP - d) % N_DP], ds.at[d], dr.at[d])
    gn_ref[...] = (jnp.sum(dpv_in[...], axis=0) / (TOK * N_DP))[0:4, :]
    for cp in sends:
        cp.wait_send()


VM = pl.BlockSpec(memory_space=pltpu.VMEM)
ANY = pl.BlockSpec(memory_space=pl.ANY)


def whole(*operands):
    sds = jax.ShapeDtypeStruct
    sem = pltpu.SemaphoreType.DMA((N_T,))
    vm = pltpu.VMEM
    return pl.pallas_call(
        body,
        name="block",
        out_shape=[sds((TOK, SHARD), bf16), sds((4, 128), f32)],
        in_specs=[VM] * 10 + [ANY] * 4,
        out_specs=[VM] * 2,
        scratch_shapes=[
            vm((N_T, TOK, SHARD), bf16),
            vm((N_T, 2 * TOK, SHARD), bf16),
            vm((N_T, TOK, SHARD), f32),
            vm((WIDTH, SHARD), bf16),
            vm((128, WIDTH), bf16),
            vm((SHARD, WIDTH), bf16),
            vm((8, TOK), f32),
            vm((N_T, 8, TOK), f32),
            vm((TOK, 128), f32),
            vm((2 * TOK, 128), f32),
            vm((2 * TOK, SHARD), f32),
            vm((128, 2 * TOK), bf16),
            vm((N_T, 16, 2 * TOK), bf16),
            vm((TOK, SHARD), bf16),
            vm((TOK, SHARD), bf16),
            vm((HEAD_DIM, TOK), bf16),
            vm((HEAD_DIM, TOK), bf16),
            vm((HEAD_DIM, TOK), bf16),
            vm((HEAD_DIM, TOK), bf16),
            vm((TOK, 128), f32),
            vm((HEADS, TOK, TOK), f32),
            vm((TOK, SHARD), bf16),
            vm((8, TOK, SHARD), bf16),
            vm((8, TOK, SHARD), bf16),
            vm((8, TOK, SHARD), bf16),
            vm((8, TOK, SHARD), bf16),
            vm((N_T, TOK, SHARD), bf16),
            vm((TOK, SHARD), f32),
            vm((TOK, SHARD), bf16),
            vm((N_T, 16, TOK), bf16),
            vm((N_T, 16, TOK), bf16),
            vm((TOK, 128), bf16),
            vm((N_T, 8, 128), f32),
            vm((N_T, 8, 128), f32),
            vm((8, 128), f32),
            vm((N_DP, 8, 128), f32),
            pltpu.SemaphoreType.DMA((4,)),
        ]
        + [sem] * 20,
        compiler_params=pltpu.CompilerParams(collective_id=1, has_side_effects=True, vmem_limit_bytes=VMEM_BYTES),
    )(*operands)


def tables():
    positions = np.arange(TOK, dtype=np.float32)
    frequency = np.exp(np.float32(-math.log(ROPE_BASE) * 2.0) * np.arange(64, dtype=np.float32) / np.float32(HEAD_DIM))
    angles = positions[:, None] * frequency[None, :].astype(np.float32)
    cosine, sine = np.cos(angles), np.sin(angles)
    return (
        np.concatenate([cosine, cosine], axis=1),
        np.concatenate([-sine, sine], axis=1),
        np.ascontiguousarray(cosine.T),
        np.ascontiguousarray(sine.T),
    )


def on_device(
    hidden_in, norm_gain, clip_base, pct_index, clip_step, w_query, w_key, w_value, w_out, doc_ids
):
    row = lambda v: v.reshape(1, WIDTH)
    tangent_shard, gn = whole(
        hidden_in, row(norm_gain), row(clip_base), row(pct_index), row(clip_step), doc_ids,
        *(jnp.asarray(t) for t in tables()),
        w_query, w_key.T, w_value.T, w_out,
    )
    return (tangent_shard, gn.reshape(SHARD))


def solution(mesh):
    in_specs = (
        P("dp", "tensor"),
        P(),
        P(),
        P(),
        P(),
        P(None, "tensor"),
        P(None, "tensor"),
        P(None, "tensor"),
        P("tensor", None),
        P("dp", None),
    )
    out_specs = (P("dp", "tensor"), P("tensor"))
    return jax.shard_map(
        on_device, mesh=mesh, in_specs=in_specs, out_specs=out_specs, check_vma=False
    )
```

time: 460 us -> 138 us (0.30)
  waiting for transfers between devices: 227 us -> 0 us
  Pallas kernels: 48.4 us -> 134 us
  blocking collectives: 84.8 us -> 0 us
  matrix products: 52.9 us -> 0 us
  local copies, waits for them, and re-layouts: 19.5 us -> 2.92 us
  between operations: 14.7 us -> 0.64 us
  other arithmetic: 11.1 us -> 0 us
    reduce_scatter x3 -> x0, waiting for transfers between devices: 169 us -> none  [the longest x1 81.1 us: on_device(): lax.psum_scatter(partial_out.astype(jnp.bfloat16), 'tensor', scatter_dime...]
    pallas_call x1, Pallas kernels: 48.4 us -> 134 us  [whole(): pl.pallas_call(body, name='block', out_shape=[sds((TOK, SHARD), bf16), sd...]
    unnamed x1 -> x0, blocking collectives: 65.1 us -> none
    all_gather x1 -> x0, waiting for transfers between devices: 58.1 us -> none  [on_device(): lax.all_gather(tangent_shard, 'tensor', axis=1, tiled=True)]
    dot_general x13 -> x0, matrix products: 51.3 us -> none  [the longest x4 31.7 us: nt(): lax.dot_general(a, b, (((1,), (1,)), ((), ())), preferred_element_type=f32)]
    psum x1 -> x0, blocking collectives: 19.8 us -> none  [on_device(): gn_product = lax.psum(channel, 'dp')]
    convert_element_type x3 -> x0, local copies, waits for them, and re-layouts: 18.4 us -> none  [the longest x2 18.3 us: on_device(): hidden = jnp.transpose(hid, (1, 0, 2)).reshape(TOK, WIDTH).astype(f32)]
    convert_element_type x4 -> x0, other arithmetic: 7.78 us -> none  [the longest x1 6.56 us: on_device(): hidden = jnp.transpose(hid, (1, 0, 2)).reshape(TOK, WIDTH).astype(f32)]
  transfers between devices with their start and end apart: 4 -> 0, of which waited for: 4 -> 0; matrix products, arithmetic and copies ran while one was open for 9% -> 0% of each run, Pallas kernels for 0% -> 0%
where the time goes in v2:
time: 138 us
  Pallas kernels  134 us (97%)
  local copies, waits for them, and re-layouts  2.92 us (2%)
    pallas_call x1, Pallas kernels, whole(): pl.pallas_call(body, name='block', out_shape=[sds((TOK, SHARD), bf16), sd...  134 us
    unnamed x2, local copies, waits for them, and re-layouts  2.92 us

profile of v2, /device:TPU:0, one launch (start us, length us, event | category | flops | bytes accessed | tf_op | source)
XLA Modules:
  0.0 137.8 jit_solution(12914943178294698047)
XLA Ops:
  0.6 134.2 %block.1 = (bf16[256,512]{1,0:T(8,128)(2,1)}, f32[4,128]{1,0:T(4,128)}) custom-call(bf16[256,512]{1,0:T(8,128)(2,1)} %x_ref.1, f32[1,8192]{1,0:T(1,128)} %bitcast.9, f32[1,8192]{1,0:T(1,128)} %bitcast.10, s32[1,8192]{1,0:T(1,128)} %bitcast.11, f32[1,8192]{1,0:T(1,128)} %bitcast.12, s32[1,256]{1,0:T(1,128)} %doc_ref.1, f32[256,128]{1,0:T(8,128)} %constant.8.clone.cos_ref, ...), custom_call_target="tpu_custom_call" | custom-call | tf_op jit(solution)/shard_map/block/pallas_call | solution.py:354
  134.8 1.7 %copy.18 = bf16[256,512]{1,0:T(8,128)(2,1)} copy(bf16[256,512]{1,0:T(8,128)(2,1)} %get-tuple-element.8) | data formatting | bytes 524288
  136.5 1.2 copy.19

commit v3 on v2

--- a/solution.py
+++ b/solution.py
@@ -28,7 +28,39 @@
 
 RELS = [(dy, dz, dc) for dy in range(N_Y) for dz in range(N_Z) for dc in range(N_C)]
 PEERS = [r for r in RELS if r != (0, 0, 0)]
-CHIPS = [(0, 0), (0, 1), (0, 3), (1, 0), (0, 2), (1, 1), (1, 3), (1, 2)]
+ROWS = {"A": (0, 128), "B": (128, 128), "0": (0, 64), "1": (64, 64), "2": (128, 64), "3": (192, 64)}
+Y, ZP, ZM = (1, 0), (0, 1), (0, 3)
+
+MOVES = [
+    ((0, 0), "B", Y), ((0, 0), "A", Y), ((0, 0), "A", ZP), ((0, 0), "A", ZM), ((0, 0), "B", ZP), ((0, 0), "B", ZM),
+    ((0, 3), "0", ZP), ((0, 1), "1", ZM), ((0, 3), "2", ZP), ((0, 1), "3", ZM), ((0, 3), "A", Y), ((0, 1), "A", Y),
+    ((1, 0), "B", ZP), ((1, 0), "B", ZM), ((1, 3), "2", ZP), ((1, 1), "3", ZM), ((0, 2), "0", Y), ((0, 2), "1", Y),
+]
+EVENTS = [
+    ([0], [12, 13], [((1, 0), 1)]),
+    ([2], [10, 6], [((0, 3), 0)]),
+    ([3], [11, 7], [((0, 1), 0)]),
+    ([1], [], [((1, 0), 0)]),
+    ([4], [8], [((0, 3), 1)]),
+    ([5], [9], [((0, 1), 1)]),
+    ([6, 7], [16, 17], [((0, 2), 0)]),
+    ([12, 13], [14, 15], [((1, 3), 1), ((1, 1), 1)]),
+    ([8, 9], [], [((0, 2), 1)]),
+    ([10, 11], [], [((1, 3), 0), ((1, 1), 0)]),
+    ([14, 15], [], [((1, 2), 1)]),
+    ([16, 17], [], [((1, 2), 0)]),
+]
+SUMS = [
+    ((1, 2), "A", Y), ((1, 1), "A", Y), ((1, 3), "A", Y), ((1, 2), "2", ZM), ((1, 2), "3", ZP),
+    ((0, 2), "0", ZM), ((0, 2), "1", ZP), ((0, 2), "2", ZM), ((0, 2), "3", ZP), ((1, 1), "B", ZP), ((1, 3), "B", ZM),
+    ((1, 0), "A", Y), ((1, 0), "B", Y), ((0, 1), "A", ZP), ((0, 3), "A", ZM), ((0, 1), "B", ZP), ((0, 3), "B", ZM),
+]
+PARTS = [(1, 2), (1, 1), (1, 3), (0, 2), (1, 0), (0, 1), (0, 3), (0, 0)]
+FIRST = {(1, 2): [0, 3, 4], (1, 1): [1], (1, 3): [2], (0, 2): [7, 8], (1, 0): [11]}
+
+
+def minus(a, b):
+    return ((a[0] - b[0]) % N_Y, (a[1] - b[1]) % N_Z)
 
 
 def ridx(rel):
@@ -74,8 +106,8 @@
     wq_hbm, wk_hbm, wv_hbm, wo_hbm,
     out_ref, gn_ref,
     hid, xs, slopes, wq, wkv, wo, ss_send, ssr, rs, kvacc, qacc, kvt, kvr, qp, qt, kp, kt, vp, vt, docs, probs, ctx,
-    pair_out, pair_in, part_out, part_in, tg, bacc, gq, gkv_out, gkv_in, gkv, gnv, gnv_in, dpv, dpv_in,
-    wsem, hs, hr, fs, sss, ssrs, kvs, kvrs, ps, pr, qs, qr, gs, gr, gf, ks, kr, ns, nr, ds, dr,
+    pair_out, pair_in, part, sums, tg, bacc, gq, gkv_out, gkv_in, gkv, gnv, gnv_in, dpv, dpv_in,
+    wsem, hs, hr, hfs, hfr, sss, ssrs, kvs, kvrs, ps, pr, qs, qr, gs, gr, gfs, gfr, ks, kr, ns, nr, ds, dr,
 ):
     me = lax.axis_index("tensor")
     dp = lax.axis_index("dp")
@@ -118,10 +150,56 @@
     for rel in PEERS:
         i = ridx(rel)
         send(ss_send, ssr.at[me], sss.at[i], ssrs.at[i], peer(me, rel))
-    send(x_ref, hid.at[me], hs.at[1], hr.at[1], sibling)
-    for dy, dz in CHIPS[1:]:
-        i = ridx((dy, dz, 0))
-        send(x_ref, hid.at[me], hs.at[i], hr.at[i], peer(me, (dy, dz, 0)))
+
+    def piece(buf, owner, rows):
+        start, size = ROWS[rows]
+        return buf.at[peer(me, owner + (0,)), pl.ds(start, size)]
+
+    def move(buf, ssem, rsem, k):
+        owner, rows, way = MOVES[k]
+        ref = piece(buf, owner, rows)
+        send(ref, ref, ssem.at[k], rsem.at[k], peer(me, way + (0,)))
+
+    def moved(buf, ssem, rsem, k):
+        owner, rows, way = MOVES[k]
+        arrived(piece(buf, minus(owner, way), rows), ssem.at[k], rsem.at[k])
+
+    def forward(buf, ssem, rsem, owner, half):
+        i = (owner[0] * N_Z + owner[1]) * 2 + half
+        ref = piece(buf, owner, "AB"[half])
+        send(ref, ref, ssem.at[i], rsem.at[i], sibling)
+
+    def gather(buf, ssem, rsem, fssem, frsem, use_half, use_block):
+        ready = [((0, 0), c, h) for c in range(N_C) for h in range(2)]
+        done = set()
+
+        def run(count):
+            for owner, core, half in ready[:count]:
+                j = peer(me, owner + (core,))
+                if core == 1:
+                    i = (owner[0] * N_Z + owner[1]) * 2 + half
+                    arrived(buf.at[j, pl.ds(half * 128, 128)], fssem.at[i], frsem.at[i])
+                use_half(j, half)
+                done.add((owner, core, half))
+                if (owner, core, 1 - half) in done:
+                    use_block(j)
+            del ready[:count]
+
+        for waits, starts, halves in EVENTS:
+            for k in waits:
+                moved(buf, ssem, rsem, k)
+            for k in starts:
+                move(buf, ssem, rsem, k)
+            for owner, half in halves:
+                forward(buf, fssem, frsem, owner, half)
+            run(2 * len(halves))
+            ready += [(owner, core, half) for core in range(N_C) for owner, half in halves]
+        run(len(ready))
+
+    for half, starts in ((1, (0, 4, 5)), (0, (1, 2, 3))):
+        for k in starts:
+            move(hid, hs, hr, k)
+        forward(hid, hfs, hfr, (0, 0), half)
     for rel in PEERS:
         i = ridx(rel)
         arrived(ssr.at[source(me, rel)], sss.at[i], ssrs.at[i])
@@ -134,47 +212,37 @@
     def lanes_of(j):
         return pl.ds(pl.multiple_of(j * SHARD, SHARD), SHARD)
 
-    def work(j):
+    def clip(j, half):
         lanes = lanes_of(j)
         thresh = base_ref[:, lanes] * (1.0 + pct_ref[:, lanes].astype(f32) / 32.0)
         over = gain_ref[:, lanes] / thresh
         step = step_ref[:, lanes]
 
         def rows_step(r, carry):
-            rows = pl.ds(pl.multiple_of(r * 32, 32), 32)
-            rest = pl.ds(pl.multiple_of(TOK + r * 32, 32), 32)
+            rows = pl.ds(pl.multiple_of(half * 128 + r * 32, 32), 32)
+            near = pl.ds(pl.multiple_of(half * 256 + r * 32, 32), 32)
+            rest = pl.ds(pl.multiple_of(half * 256 + 128 + r * 32, 32), 32)
             x = hid[j, rows, :].astype(f32)
             scale = rs[rows, :]
             for l in range(SHARD // 128):
                 cut = slice(l * 128, l * 128 + 128)
                 ratio = x[:, cut] * scale * over[:, cut]
                 bent = jnp.tanh(ratio)
-                xs[j, rows, cut] = (thresh[:, cut] * bent).astype(bf16)
+                xs[j, near, cut] = (thresh[:, cut] * bent).astype(bf16)
                 slope = bent - ratio * (1.0 - bent * bent)
                 slopes[j, rows, cut] = slope
                 xs[j, rest, cut] = (slope * step[:, cut]).astype(bf16)
             return carry
 
-        lax.fori_loop(0, TOK // 32, rows_step, 0)
-        kvacc[...] += nt(xs[j], wkv[:, lanes])
+        lax.fori_loop(0, 4, rows_step, 0)
+
+    def project(j):
+        kvacc[...] += nt(xs[j], wkv[:, lanes_of(j)])
 
     loads[0].wait()
     loads[1].wait()
 
-    def gather(buf, ssem, rsem, fsem, use):
-        for dy, dz in CHIPS:
-            j = source(me, (dy, dz, 0))
-            i1 = ridx((dy, dz, 1))
-            if (dy, dz) != (0, 0):
-                i = ridx((dy, dz, 0))
-                arrived(buf.at[j], ssem.at[i], rsem.at[i])
-                send(buf.at[j], buf.at[j], fsem.at[i1], rsem.at[i1], sibling)
-            use(j)
-            j1 = source(me, (dy, dz, 1))
-            arrived(buf.at[j1], ssem.at[i1], rsem.at[i1])
-            use(j1)
-
-    gather(hid, hs, hr, fs, work)
+    gather(hid, hs, hr, hfs, hfr, clip, project)
 
     kvt[...] = nt(permutation(), kvacc[...].astype(bf16)).astype(bf16)
 
@@ -197,9 +265,11 @@
     lax.fori_loop(0, N_T, q_step, 0)
     for h in range(HEADS):
         cut = slice(h * 128, h * 128 + 128)
-        for out, top in ((qp, 0), (qt, TOK)):
-            z = qacc[pl.ds(top, TOK), cut]
-            out[:, cut] = (z * cos_ref[...] + pltpu.roll(z, 64, 1) * sin_ref[...]).astype(bf16)
+        for half in range(2):
+            rows = pl.ds(half * 128, 128)
+            for out, top in ((qp, 0), (qt, 128)):
+                z = qacc[pl.ds(half * 256 + top, 128), cut]
+                out[rows, cut] = (z * cos_ref[rows, :] + pltpu.roll(z, 64, 1) * sin_ref[rows, :]).astype(bf16)
 
     for rel in PEERS:
         i = ridx(rel)
@@ -207,11 +277,12 @@
     both = kvr[...].astype(f32)
     keys = both[:, 0:8, :].reshape(HEAD_DIM, 2 * TOK)
     vals = both[:, 8:16, :].reshape(HEAD_DIM, 2 * TOK).astype(bf16)
-    vp[...] = vals[:, :TOK]
-    vt[...] = vals[:, TOK:]
+    for half in range(2):
+        vp[:, half * 128 : half * 128 + 128] = vals[:, half * 256 : half * 256 + 128]
+        vt[:, half * 128 : half * 128 + 128] = vals[:, half * 256 + 128 : half * 256 + 256]
     cost, sint = cost_ref[...], sint_ref[...]
-    for out, left in ((kp, 0), (kt, TOK)):
-        z = keys[:, left : left + TOK]
+    for out, left in ((kp, 0), (kt, 128)):
+        z = jnp.concatenate([keys[:, left : left + 128], keys[:, left + 256 : left + 384]], axis=1)
         front, back = z[:64], z[64:]
         out[0:64, :] = (front * cost - back * sint).astype(bf16)
         out[64:128, :] = (back * cost + front * sint).astype(bf16)
@@ -236,21 +307,44 @@
         ctx[:, cut] = (nt(tan, vp[...]) + nt(prob.astype(bf16), vt[...])).astype(bf16)
 
     loads[3].wait()
-    order = CHIPS[::-1]
+
+    def slot(chip):
+        return chip[0] * N_Z + chip[1]
 
     def pair_part(s):
-        dy, dz = order[s]
-        pair_out[s] = dot(ctx[...], wo[:, lanes_of(peer(me, (dy, dz, 1)))]).astype(bf16)
-        send(pair_out.at[s], pair_in.at[s], ps.at[s], pr.at[s], sibling)
+        i = slot(PARTS[s])
+        pair_out[i] = dot(ctx[...], wo[:, lanes_of(peer(me, PARTS[s] + (1,)))]).astype(bf16)
+        send(pair_out.at[i], pair_in.at[i], ps.at[i], pr.at[i], sibling)
+
+    def give(k):
+        chip, rows, way = SUMS[k]
+        start, size = ROWS[rows]
+        send(part.at[slot(chip), pl.ds(start, size)], sums.at[k, pl.ds(0, size)], qs.at[k], qr.at[k], peer(me, way + (0,)))
 
     def own_part(s):
-        dy, dz = order[s]
-        to = peer(me, (dy, dz, 0))
-        mine = dot(ctx[...], wo[:, lanes_of(to)]).astype(bf16).astype(f32)
-        arrived(pair_in.at[s], ps.at[s], pr.at[s])
-        part_out[s] = (mine + pair_in[s].astype(f32)).astype(bf16)
-        if s < 7:
-            send(part_out.at[s], part_in.at[s], qs.at[s], qr.at[s], to)
+        i = slot(PARTS[s])
+        mine = dot(ctx[...], wo[:, lanes_of(peer(me, PARTS[s] + (0,)))]).astype(bf16).astype(f32)
+        arrived(pair_in.at[i], ps.at[i], pr.at[i])
+        part[i] = (mine + pair_in[i].astype(f32)).astype(bf16)
+        for k in FIRST.get(PARTS[s], ()):
+            give(k)
+
+    def add(rows, into, *parts):
+        chip, out = into
+        start, size = ROWS[rows]
+        for k in parts:
+            arrived(sums.at[k, pl.ds(0, ROWS[SUMS[k][1]][1])], qs.at[k], qr.at[k])
+        value = part[slot(chip), pl.ds(start, size), :].astype(f32)
+        for k in parts:
+            low = start - ROWS[SUMS[k][1]][0]
+            value = value + sums[k, pl.ds(low, size), :].astype(f32)
+        if out is None:
+            part[slot(chip), pl.ds(start, size), :] = value.astype(bf16)
+        else:
+            out[me, pl.ds(start, size), :] = value.astype(bf16)
+
+    def take(rows, chip, *parts):
+        add(rows, (chip, None), *parts)
 
     pair_part(0)
     pair_part(1)
@@ -258,29 +352,41 @@
         if s + 2 < 8:
             pair_part(s + 2)
         own_part(s)
-    for s in range(7):
-        arrived(part_in.at[s], qs.at[s], qr.at[s])
-
-    def sum_step(r, carry):
-        rows = pl.ds(pl.multiple_of(r * 32, 32), 32)
-        value = part_out[7, rows, :].astype(f32)
-        for s in range(7):
-            value = value + part_in[s, rows, :].astype(f32)
-        tg[me, rows, :] = value.astype(bf16)
-        return carry
-
-    lax.fori_loop(0, TOK // 32, sum_step, 0)
-    send(tg.at[me], tg.at[me], gs.at[1], gr.at[1], sibling)
-    for dy, dz in CHIPS[1:]:
-        i = ridx((dy, dz, 0))
-        send(tg.at[me], tg.at[me], gs.at[i], gr.at[i], peer(me, (dy, dz, 0)))
+        if s == 5:
+            take("2", (1, 3), 3)
+            give(10)
+            take("3", (1, 1), 4)
+            give(9)
+    take("A", (0, 2), 0)
+    give(5)
+    give(6)
+    take("2", (0, 3), 7)
+    give(16)
+    take("3", (0, 1), 8)
+    give(15)
+    take("B", (1, 0), 9, 10)
+    give(12)
+    take("1", (0, 1), 6)
+    take("A", (0, 1), 1)
+    give(13)
+    take("0", (0, 3), 5)
+    take("A", (0, 3), 2)
+    give(14)
+    add("B", ((0, 0), tg), 12, 15, 16)
+    for k in (0, 4, 5):
+        move(tg, gs, gr, k)
+    forward(tg, gfs, gfr, (0, 0), 1)
+    add("A", ((0, 0), tg), 11, 13, 14)
+    for k in (1, 2, 3):
+        move(tg, gs, gr, k)
+    forward(tg, gfs, gfr, (0, 0), 0)
     out_ref[...] = tg[me]
     bacc[...] = jnp.zeros_like(bacc)
 
     def back(j):
         bacc[...] += nt(tg[j], wo[:, lanes_of(j)])
 
-    gather(tg, gs, gr, gf, back)
+    gather(tg, gs, gr, gfs, gfr, lambda j, half: None, back)
 
     gk = jnp.zeros((HEAD_DIM, TOK), f32)
     gv = jnp.zeros((HEAD_DIM, TOK), f32)
@@ -349,7 +455,7 @@
 
 def whole(*operands):
     sds = jax.ShapeDtypeStruct
-    sem = pltpu.SemaphoreType.DMA((N_T,))
+    sem = pltpu.SemaphoreType.DMA((18,))
     vm = pltpu.VMEM
     return pl.pallas_call(
         body,
@@ -383,7 +489,7 @@
             vm((8, TOK, SHARD), bf16),
             vm((8, TOK, SHARD), bf16),
             vm((8, TOK, SHARD), bf16),
-            vm((8, TOK, SHARD), bf16),
+            vm((len(SUMS), 128, SHARD), bf16),
             vm((N_T, TOK, SHARD), bf16),
             vm((TOK, SHARD), f32),
             vm((TOK, SHARD), bf16),
@@ -396,7 +502,7 @@
             vm((N_DP, 8, 128), f32),
             pltpu.SemaphoreType.DMA((4,)),
         ]
-        + [sem] * 20,
+        + [sem] * 22,
         compiler_params=pltpu.CompilerParams(collective_id=1, has_side_effects=True, vmem_limit_bytes=VMEM_BYTES),
     )(*operands)
 

time: 138 us -> 107 us (0.78)
  Pallas kernels: 134 us -> 103 us
    pallas_call x1, Pallas kernels: 134 us -> 103 us  [whole(): pl.pallas_call(body, name='block', out_shape=[sds((TOK, SHARD), bf16), sd...]
where the time goes in v3:
time: 107 us
  Pallas kernels  103 us (96%)
  local copies, waits for them, and re-layouts  2.92 us (3%)
    pallas_call x1, Pallas kernels, whole(): pl.pallas_call(body, name='block', out_shape=[sds((TOK, SHARD), bf16), sd...  103 us
    unnamed x2, local copies, waits for them, and re-layouts  2.92 us

profile of v3, /device:TPU:0, one launch (start us, length us, event | category | flops | bytes accessed | tf_op | source)
XLA Modules:
  0.0 106.8 jit_solution(14436779025038205273)
XLA Ops:
  0.6 103.2 %block.1 = (bf16[256,512]{1,0:T(8,128)(2,1)}, f32[4,128]{1,0:T(4,128)}) custom-call(bf16[256,512]{1,0:T(8,128)(2,1)} %x_ref.1, f32[1,8192]{1,0:T(1,128)} %bitcast.9, f32[1,8192]{1,0:T(1,128)} %bitcast.10, s32[1,8192]{1,0:T(1,128)} %bitcast.11, f32[1,8192]{1,0:T(1,128)} %bitcast.12, s32[1,256]{1,0:T(1,128)} %doc_ref.1, f32[256,128]{1,0:T(8,128)} %constant.8.clone.cos_ref, ...), custom_call_target="tpu_custom_call" | custom-call | tf_op jit(solution)/shard_map/block/pallas_call | solution.py:460
  103.9 1.7 %copy.18 = bf16[256,512]{1,0:T(8,128)(2,1)} copy(bf16[256,512]{1,0:T(8,128)(2,1)} %get-tuple-element.8) | data formatting | bytes 524288
  105.5 1.2 %copy.19 = f32[512]{0:T(512)} copy(f32[512]{0:T(512)} %bitcast.13) | data formatting | bytes 4096

commit v4 on v3

--- a/solution.py
+++ b/solution.py
@@ -25,6 +25,7 @@
 HEADS = 4
 N_DP = 8
 VMEM_BYTES = 60 << 20
+LATE = 16
 
 RELS = [(dy, dz, dc) for dy in range(N_Y) for dz in range(N_Z) for dc in range(N_C)]
 PEERS = [r for r in RELS if r != (0, 0, 0)]
@@ -102,9 +103,10 @@
 
 
 def body(
-    x_ref, gain_ref, base_ref, pct_ref, step_ref, doc_ref, cos_ref, sin_ref, cost_ref, sint_ref,
+    x_hbm, gain_hbm, base_hbm, pct_hbm, step_hbm, doc_hbm, cos_hbm, sin_hbm, cost_hbm, sint_hbm,
     wq_hbm, wk_hbm, wv_hbm, wo_hbm,
-    out_ref, gn_ref,
+    out_hbm, gn_ref,
+    gain_ref, base_ref, pct_ref, step_ref, doc_ref, cos_ref, sin_ref, cost_ref, sint_ref,
     hid, xs, slopes, wq, wkv, wo, ss_send, ssr, rs, kvacc, qacc, kvt, kvr, qp, qt, kp, kt, vp, vt, docs, probs, ctx,
     pair_out, pair_in, part, sums, tg, bacc, gq, gkv_out, gkv_in, gkv, gnv, gnv_in, dpv, dpv_in,
     wsem, hs, hr, hfs, hfr, sss, ssrs, kvs, kvrs, ps, pr, qs, qr, gs, gr, gfs, gfr, ks, kr, ns, nr, ds, dr,
@@ -117,6 +119,13 @@
         pl.semaphore_signal(barrier, inc=1, device_id=(dp, peer(me, rel)), device_id_type=MESH)
     for d in range(1, N_DP):
         pl.semaphore_signal(barrier, inc=1, device_id=((dp + d) % N_DP, me), device_id_type=MESH)
+    copies = [
+        (x_hbm, hid.at[me]), (doc_hbm, doc_ref), (gain_hbm, gain_ref), (base_hbm, base_ref), (pct_hbm, pct_ref),
+        (step_hbm, step_ref), (cos_hbm, cos_ref), (sin_hbm, sin_ref), (cost_hbm, cost_ref), (sint_hbm, sint_ref),
+    ]
+    small = [pltpu.make_async_copy(a, b, wsem.at[4 + i]) for i, (a, b) in enumerate(copies)]
+    for load in small:
+        load.start()
     loads = [
         pltpu.make_async_copy(wk_hbm, wkv.at[pl.ds(0, 64)], wsem.at[0]),
         pltpu.make_async_copy(wv_hbm, wkv.at[pl.ds(64, 64)], wsem.at[1]),
@@ -136,14 +145,16 @@
     def arrived(dst, ssem, rsem):
         remote(dst, dst, ssem, rsem, dp, me).wait_recv()
 
-    own = x_ref[...].astype(f32)
+    small[0].wait()
+    own = hid[me].astype(f32)
     square = own * own
     high = square.astype(bf16)
     low = (square - high.astype(f32)).astype(bf16)
     ones = jnp.ones((8, SHARD), bf16)
     ss_send[...] = nt(ones, high) + nt(ones, low)
     ssr[me] = ss_send[...]
-    hid[me] = x_ref[...]
+    for load in small[1:]:
+        load.wait()
     docs[...] = jnp.transpose(jnp.broadcast_to(doc_ref[...].astype(f32), (128, TOK)))
 
     pl.semaphore_wait(barrier, len(PEERS) + N_DP - 1)
@@ -169,7 +180,7 @@
         ref = piece(buf, owner, "AB"[half])
         send(ref, ref, ssem.at[i], rsem.at[i], sibling)
 
-    def gather(buf, ssem, rsem, fssem, frsem, use_half, use_block):
+    def gather(buf, ssem, rsem, fssem, frsem, use_half, use_block, before):
         ready = [((0, 0), c, h) for c in range(N_C) for h in range(2)]
         done = set()
 
@@ -185,14 +196,19 @@
                     use_block(j)
             del ready[:count]
 
-        for waits, starts, halves in EVENTS:
+        for step, (waits, starts, halves) in enumerate(EVENTS):
             for k in waits:
                 moved(buf, ssem, rsem, k)
             for k in starts:
                 move(buf, ssem, rsem, k)
             for owner, half in halves:
                 forward(buf, fssem, frsem, owner, half)
-            run(2 * len(halves))
+            if before is not None and step < 2:
+                ready += [(owner, core, half) for core in range(N_C) for owner, half in halves]
+                continue
+            if before is not None and step == 2:
+                before()
+            run(2 * len(halves) + (4 if 2 <= step < 8 and before is not None else 0))
             ready += [(owner, core, half) for core in range(N_C) for owner, half in halves]
         run(len(ready))
 
@@ -200,14 +216,8 @@
         for k in starts:
             move(hid, hs, hr, k)
         forward(hid, hfs, hfr, (0, 0), half)
-    for rel in PEERS:
-        i = ridx(rel)
-        arrived(ssr.at[source(me, rel)], sss.at[i], ssrs.at[i])
-    total = jnp.sum(ssr[...], axis=0)
-    scale = lax.rsqrt(total / WIDTH + EPSILON)
-    rs[...] = jnp.transpose(jnp.broadcast_to(scale[0:1, :], (128, TOK)))
-
     kvacc[...] = jnp.zeros_like(kvacc)
+    qacc[...] = jnp.zeros_like(qacc)
 
     def lanes_of(j):
         return pl.ds(pl.multiple_of(j * SHARD, SHARD), SHARD)
@@ -218,31 +228,44 @@
         over = gain_ref[:, lanes] / thresh
         step = step_ref[:, lanes]
 
-        def rows_step(r, carry):
-            rows = pl.ds(pl.multiple_of(half * 128 + r * 32, 32), 32)
-            near = pl.ds(pl.multiple_of(half * 256 + r * 32, 32), 32)
-            rest = pl.ds(pl.multiple_of(half * 256 + 128 + r * 32, 32), 32)
-            x = hid[j, rows, :].astype(f32)
-            scale = rs[rows, :]
-            for l in range(SHARD // 128):
-                cut = slice(l * 128, l * 128 + 128)
-                ratio = x[:, cut] * scale * over[:, cut]
-                bent = jnp.tanh(ratio)
-                xs[j, near, cut] = (thresh[:, cut] * bent).astype(bf16)
-                slope = bent - ratio * (1.0 - bent * bent)
-                slopes[j, rows, cut] = slope
-                xs[j, rest, cut] = (slope * step[:, cut]).astype(bf16)
-            return carry
-
-        lax.fori_loop(0, 4, rows_step, 0)
+        rows = pl.ds(half * 128, 128)
+        near = pl.ds(half * 256, 128)
+        rest = pl.ds(half * 256 + 128, 128)
+        x = hid[j, rows, :].astype(f32)
+        scale = rs[rows, :]
+        for l in range(SHARD // 128):
+            cut = slice(l * 128, l * 128 + 128)
+            ratio = x[:, cut] * scale * over[:, cut]
+            bent = jnp.tanh(ratio)
+            xs[j, near, cut] = (thresh[:, cut] * bent).astype(bf16)
+            slope = bent - ratio * (1.0 - bent * bent)
+            slopes[j, rows, cut] = slope
+            xs[j, rest, cut] = (slope * step[:, cut]).astype(bf16)
+
+    late = []
+
+    def query(j):
+        qacc[...] += jnp.dot(xs[j], wq[lanes_of(j), :], preferred_element_type=f32)
 
     def project(j):
         kvacc[...] += nt(xs[j], wkv[:, lanes_of(j)])
-
-    loads[0].wait()
-    loads[1].wait()
-
-    gather(hid, hs, hr, hfs, hfr, clip, project)
+        late.append(j)
+        if len(late) > LATE:
+            query(late.pop(0))
+
+
+    def norms():
+        for rel in PEERS:
+            i = ridx(rel)
+            arrived(ssr.at[source(me, rel)], sss.at[i], ssrs.at[i])
+        total = jnp.sum(ssr[...], axis=0)
+        scale = lax.rsqrt(total / WIDTH + EPSILON)
+        rs[...] = jnp.transpose(jnp.broadcast_to(scale[0:1, :], (128, TOK)))
+
+        for load in loads[:3]:
+            load.wait()
+
+    gather(hid, hs, hr, hfs, hfr, clip, project, norms)
 
     kvt[...] = nt(permutation(), kvacc[...].astype(bf16)).astype(bf16)
 
@@ -255,14 +278,8 @@
         to = peer(me, rel)
         send(kvt.at[block(to // N_C)], kvr.at[me], kvs.at[i], kvrs.at[i], to)
 
-    loads[2].wait()
-    qacc[...] = jnp.zeros_like(qacc)
-
-    def q_step(j, carry):
-        qacc[...] += jnp.dot(xs[j], wq[lanes_of(j), :], preferred_element_type=f32)
-        return carry
-
-    lax.fori_loop(0, N_T, q_step, 0)
+    for j in late:
+        query(j)
     for h in range(HEADS):
         cut = slice(h * 128, h * 128 + 128)
         for half in range(2):
@@ -380,34 +397,39 @@
     for k in (1, 2, 3):
         move(tg, gs, gr, k)
     forward(tg, gfs, gfr, (0, 0), 0)
-    out_ref[...] = tg[me]
+    result = pltpu.make_async_copy(tg.at[me], out_hbm, wsem.at[0])
+    result.start()
     bacc[...] = jnp.zeros_like(bacc)
 
     def back(j):
         bacc[...] += nt(tg[j], wo[:, lanes_of(j)])
 
-    gather(tg, gs, gr, gfs, gfr, lambda j, half: None, back)
+    gather(tg, gs, gr, gfs, gfr, lambda j, half: None, back, None)
 
     gk = jnp.zeros((HEAD_DIM, TOK), f32)
     gv = jnp.zeros((HEAD_DIM, TOK), f32)
+    marks = []
     for h in range(HEADS):
         cut = slice(h * 128, h * 128 + 128)
         bc = bacc[:, cut].astype(bf16)
         prob = probs[h]
         g = dot(bc, vp[...])
         score = (prob * (g - jnp.sum(prob * g, axis=1, keepdims=True)) * score_scale).astype(bf16)
-        z = nt(score, kp[...])
-        gq[:, cut] = (z * cos_ref[...] - pltpu.roll(z, 64, 1) * sin_ref[...]).astype(bf16)
+        marks.append(score)
         gk = gk + tn(qp[:, cut], score)
         gv = gv + tn(bc, prob.astype(bf16))
     front, back_half = gk[:64], gk[64:]
     gk = jnp.concatenate([front * cost + back_half * sint, back_half * cost - front * sint], axis=0)
     gkv_out[...] = jnp.concatenate([gk.reshape(N_T, 8, TOK), gv.reshape(N_T, 8, TOK)], axis=1).astype(bf16)
-    gkv_in[me] = gkv_out[me]
-    for rel in PEERS:
+    for rel in PEERS[::-1]:
         i = ridx(rel)
         to = peer(me, rel)
         send(gkv_out.at[to], gkv_in.at[me], ks.at[i], kr.at[i], to)
+    gkv_in[me] = gkv_out[me]
+    for h in range(HEADS):
+        cut = slice(h * 128, h * 128 + 128)
+        z = nt(marks[h], kp[...])
+        gq[:, cut] = (z * cos_ref[...] - pltpu.roll(z, 64, 1) * sin_ref[...]).astype(bf16)
 
     def column_sums(product):
         line = jnp.sum(product, axis=0, keepdims=True)
@@ -417,7 +439,7 @@
         gnv[j] = column_sums(nt(gq[...], wq[lanes_of(j), :]) * slopes[j])
         return carry
 
-    lax.fori_loop(0, N_T, query_step, 0)
+    lax.fori_loop(0, N_T, query_step, 0, unroll=4)
     for rel in PEERS:
         i = ridx(rel)
         arrived(gkv_in.at[source(me, rel)], ks.at[i], kr.at[i])
@@ -429,7 +451,7 @@
         gnv[j] += column_sums(dot(gkv[...], wkv[:, lanes_of(j)]) * slopes[j])
         return carry
 
-    lax.fori_loop(0, N_T, key_step, 0)
+    lax.fori_loop(0, N_T, key_step, 0, unroll=4)
     gnv_in[me] = gnv[me]
     for rel in PEERS:
         i = ridx(rel)
@@ -444,7 +466,8 @@
         send(dpv, dpv_in.at[dp], ds.at[d], dr.at[d], me, (dp + d) % N_DP)
     for d in range(1, N_DP):
         arrived(dpv_in.at[(dp + N_DP - d) % N_DP], ds.at[d], dr.at[d])
-    gn_ref[...] = (jnp.sum(dpv_in[...], axis=0) / (TOK * N_DP))[0:4, :]
+    gn_ref[...] = jnp.sum(dpv_in[...], axis=0)[0:4, :]
+    result.wait()
     for cp in sends:
         cp.wait_send()
 
@@ -461,9 +484,18 @@
         body,
         name="block",
         out_shape=[sds((TOK, SHARD), bf16), sds((4, 128), f32)],
-        in_specs=[VM] * 10 + [ANY] * 4,
-        out_specs=[VM] * 2,
+        in_specs=[ANY] * 14,
+        out_specs=[ANY, VM],
         scratch_shapes=[
+            vm((1, WIDTH), f32),
+            vm((1, WIDTH), f32),
+            vm((1, WIDTH), jnp.int32),
+            vm((1, WIDTH), f32),
+            vm((1, TOK), jnp.int32),
+            vm((TOK, 128), f32),
+            vm((TOK, 128), f32),
+            vm((64, TOK), f32),
+            vm((64, TOK), f32),
             vm((N_T, TOK, SHARD), bf16),
             vm((N_T, 2 * TOK, SHARD), bf16),
             vm((N_T, TOK, SHARD), f32),
@@ -500,11 +532,27 @@
             vm((N_T, 8, 128), f32),
             vm((8, 128), f32),
             vm((N_DP, 8, 128), f32),
-            pltpu.SemaphoreType.DMA((4,)),
+            pltpu.SemaphoreType.DMA((14,)),
         ]
         + [sem] * 22,
         compiler_params=pltpu.CompilerParams(collective_id=1, has_side_effects=True, vmem_limit_bytes=VMEM_BYTES),
     )(*operands)
+
+
+def finish_body(shard_ref, gn_ref, out_ref, mean_ref):
+    out_ref[...] = shard_ref[...]
+    mean_ref[...] = gn_ref[...] / (TOK * N_DP)
+
+
+def finish(shard, gn):
+    sds = jax.ShapeDtypeStruct
+    return pl.pallas_call(
+        finish_body,
+        name="finish",
+        out_shape=[sds((TOK, SHARD), bf16), sds((4, 128), f32)],
+        in_specs=[VM] * 2,
+        out_specs=[VM] * 2,
+    )(shard, gn)
 
 
 def tables():
@@ -529,6 +577,7 @@
         *(jnp.asarray(t) for t in tables()),
         w_query, w_key.T, w_value.T, w_out,
     )
+    tangent_shard, gn = finish(tangent_shard, gn)
     return (tangent_shard, gn.reshape(SHARD))
 
 

time: 107 us -> 101 us (0.944)
  Pallas kernels: 103 us -> 100 us
  local copies, waits for them, and re-layouts: 2.92 us -> 0 us
    pallas_call x1, Pallas kernels: 103 us -> 98.6 us  [whole(): pl.pallas_call(body, name='block', out_shape=[sds((TOK, SHARD), bf16), sd...]
    unnamed x2 -> x0, local copies, waits for them, and re-layouts: 2.92 us -> none
    pallas_call x0 -> x1, Pallas kernels: none -> 1.68 us  [finish(): pl.pallas_call(finish_body, name='finish', out_shape=[sds((TOK, SHARD), b...]
where the time goes in v4:
time: 101 us
  Pallas kernels  100 us (99%)
    pallas_call x1, Pallas kernels, whole(): pl.pallas_call(body, name='block', out_shape=[sds((TOK, SHARD), bf16), sd...  98.6 us

profile of v4, /device:TPU:0, one launch (start us, length us, event | category | flops | bytes accessed | tf_op | source)
XLA Modules:
  0.0 100.9 jit_solution(11564439615441037481)
XLA Ops:
  0.6 98.6 %block.1 = (bf16[256,512]{1,0:T(8,128)(2,1)}, f32[4,128]{1,0:T(4,128)}) custom-call(bf16[256,512]{1,0:T(8,128)(2,1)} %x_hbm.1, f32[1,8192]{1,0:T(1,128)} %bitcast.9, f32[1,8192]{1,0:T(1,128)} %bitcast.10, s32[1,8192]{1,0:T(1,128)} %bitcast.11, f32[1,8192]{1,0:T(1,128)} %bitcast.12, s32[1,256]{1,0:T(1,128)} %doc_hbm.1, f32[256,128]{1,0:T(8,128)} %constant.8.clone.cos_hbm, ...), custom_call_target="tpu_custom_call" | custom-call | tf_op jit(solution)/shard_map/block/pallas_call | solution.py:483
  99.2 1.7 %finish.1 = (bf16[256,512]{1,0:T(8,128)(2,1)}, f32[4,128]{1,0:T(4,128)}) custom-call(bf16[256,512]{1,0:T(8,128)(2,1)} %get-tuple-element.6.shard_ref, f32[4,128]{1,0:T(4,128)} %get-tuple-element.7.gn_ref), custom_call_target="tpu_custom_call" | custom-call | tf_op jit(solution)/shard_map/finish/pallas_call | solution.py:549

commit v5 on v4

--- a/solution.py
+++ b/solution.py
@@ -25,11 +25,10 @@
 HEADS = 4
 N_DP = 8
 VMEM_BYTES = 60 << 20
-LATE = 16
 
 RELS = [(dy, dz, dc) for dy in range(N_Y) for dz in range(N_Z) for dc in range(N_C)]
 PEERS = [r for r in RELS if r != (0, 0, 0)]
-ROWS = {"A": (0, 128), "B": (128, 128), "0": (0, 64), "1": (64, 64), "2": (128, 64), "3": (192, 64)}
+ROWS = {"A": (0, 112), "B": (112, 144), "0": (0, 48), "1": (48, 64), "2": (112, 80), "3": (192, 64)}
 Y, ZP, ZM = (1, 0), (0, 1), (0, 3)
 
 MOVES = [
@@ -58,6 +57,8 @@
 ]
 PARTS = [(1, 2), (1, 1), (1, 3), (0, 2), (1, 0), (0, 1), (0, 3), (0, 0)]
 FIRST = {(1, 2): [0, 3, 4], (1, 1): [1], (1, 3): [2], (0, 2): [7, 8], (1, 0): [11]}
+
+FAR = [chip + (core,) for chip in PARTS for core in (1, 0)][:-1]
 
 
 def minus(a, b):
@@ -158,7 +159,7 @@
     docs[...] = jnp.transpose(jnp.broadcast_to(doc_ref[...].astype(f32), (128, TOK)))
 
     pl.semaphore_wait(barrier, len(PEERS) + N_DP - 1)
-    for rel in PEERS:
+    for rel in FAR:
         i = ridx(rel)
         send(ss_send, ssr.at[me], sss.at[i], ssrs.at[i], peer(me, rel))
 
@@ -189,7 +190,7 @@
                 j = peer(me, owner + (core,))
                 if core == 1:
                     i = (owner[0] * N_Z + owner[1]) * 2 + half
-                    arrived(buf.at[j, pl.ds(half * 128, 128)], fssem.at[i], frsem.at[i])
+                    arrived(buf.at[j, pl.ds(*ROWS["AB"[half]])], fssem.at[i], frsem.at[i])
                 use_half(j, half)
                 done.add((owner, core, half))
                 if (owner, core, 1 - half) in done:
@@ -212,9 +213,9 @@
             ready += [(owner, core, half) for core in range(N_C) for owner, half in halves]
         run(len(ready))
 
-    for half, starts in ((1, (0, 4, 5)), (0, (1, 2, 3))):
-        for k in starts:
-            move(hid, hs, hr, k)
+    for k in (0, 2, 3, 1, 4, 5):
+        move(hid, hs, hr, k)
+    for half in range(2):
         forward(hid, hfs, hfr, (0, 0), half)
     kvacc[...] = jnp.zeros_like(kvacc)
     qacc[...] = jnp.zeros_like(qacc)
@@ -228,30 +229,22 @@
         over = gain_ref[:, lanes] / thresh
         step = step_ref[:, lanes]
 
-        rows = pl.ds(half * 128, 128)
-        near = pl.ds(half * 256, 128)
-        rest = pl.ds(half * 256 + 128, 128)
+        start, size = ROWS["AB"[half]]
+        rows = pl.ds(start, size)
+        rest = pl.ds(TOK + start, size)
         x = hid[j, rows, :].astype(f32)
         scale = rs[rows, :]
         for l in range(SHARD // 128):
             cut = slice(l * 128, l * 128 + 128)
             ratio = x[:, cut] * scale * over[:, cut]
             bent = jnp.tanh(ratio)
-            xs[j, near, cut] = (thresh[:, cut] * bent).astype(bf16)
+            xs[j, rows, cut] = (thresh[:, cut] * bent).astype(bf16)
             slope = bent - ratio * (1.0 - bent * bent)
             slopes[j, rows, cut] = slope
             xs[j, rest, cut] = (slope * step[:, cut]).astype(bf16)
 
-    late = []
-
-    def query(j):
-        qacc[...] += jnp.dot(xs[j], wq[lanes_of(j), :], preferred_element_type=f32)
-
     def project(j):
         kvacc[...] += nt(xs[j], wkv[:, lanes_of(j)])
-        late.append(j)
-        if len(late) > LATE:
-            query(late.pop(0))
 
 
     def norms():
@@ -262,7 +255,7 @@
         scale = lax.rsqrt(total / WIDTH + EPSILON)
         rs[...] = jnp.transpose(jnp.broadcast_to(scale[0:1, :], (128, TOK)))
 
-        for load in loads[:3]:
+        for load in loads[:2]:
             load.wait()
 
     gather(hid, hs, hr, hfs, hfr, clip, project, norms)
@@ -273,20 +266,26 @@
         return pl.ds(pl.multiple_of(chip * 16, 16), 16)
 
     kvr[me] = kvt[block(me // N_C), :]
-    for rel in PEERS:
+    for rel in FAR:
         i = ridx(rel)
         to = peer(me, rel)
         send(kvt.at[block(to // N_C)], kvr.at[me], kvs.at[i], kvrs.at[i], to)
 
-    for j in late:
-        query(j)
+    def query_four(r, carry):
+        value = qacc[...]
+        for i in range(4):
+            j = r * 4 + i
+            value = value + jnp.dot(xs[j], wq[lanes_of(j), :], preferred_element_type=f32)
+        qacc[...] = value
+        return carry
+
+    loads[2].wait()
+    lax.fori_loop(0, N_T // 4, query_four, 0)
     for h in range(HEADS):
         cut = slice(h * 128, h * 128 + 128)
-        for half in range(2):
-            rows = pl.ds(half * 128, 128)
-            for out, top in ((qp, 0), (qt, 128)):
-                z = qacc[pl.ds(half * 256 + top, 128), cut]
-                out[rows, cut] = (z * cos_ref[rows, :] + pltpu.roll(z, 64, 1) * sin_ref[rows, :]).astype(bf16)
+        for out, top in ((qp, 0), (qt, TOK)):
+            z = qacc[pl.ds(top, TOK), cut]
+            out[:, cut] = (z * cos_ref[...] + pltpu.roll(z, 64, 1) * sin_ref[...]).astype(bf16)
 
     for rel in PEERS:
         i = ridx(rel)
@@ -294,12 +293,11 @@
     both = kvr[...].astype(f32)
     keys = both[:, 0:8, :].reshape(HEAD_DIM, 2 * TOK)
     vals = both[:, 8:16, :].reshape(HEAD_DIM, 2 * TOK).astype(bf16)
-    for half in range(2):
-        vp[:, half * 128 : half * 128 + 128] = vals[:, half * 256 : half * 256 + 128]
-        vt[:, half * 128 : half * 128 + 128] = vals[:, half * 256 + 128 : half * 256 + 256]
+    vp[...] = vals[:, :TOK]
+    vt[...] = vals[:, TOK:]
     cost, sint = cost_ref[...], sint_ref[...]
-    for out, left in ((kp, 0), (kt, 128)):
-        z = jnp.concatenate([keys[:, left : left + 128], keys[:, left + 256 : left + 384]], axis=1)
+    for out, left in ((kp, 0), (kt, TOK)):
+        z = keys[:, left : left + TOK]
         front, back = z[:64], z[64:]
         out[0:64, :] = (front * cost - back * sint).astype(bf16)
         out[64:128, :] = (back * cost + front * sint).astype(bf16)
@@ -390,13 +388,12 @@
     take("A", (0, 3), 2)
     give(14)
     add("B", ((0, 0), tg), 12, 15, 16)
-    for k in (0, 4, 5):
+    move(tg, gs, gr, 0)
+    add("A", ((0, 0), tg), 11, 13, 14)
+    for k in (2, 3, 1, 4, 5):
         move(tg, gs, gr, k)
-    forward(tg, gfs, gfr, (0, 0), 1)
-    add("A", ((0, 0), tg), 11, 13, 14)
-    for k in (1, 2, 3):
-        move(tg, gs, gr, k)
-    forward(tg, gfs, gfr, (0, 0), 0)
+    for half in range(2):
+        forward(tg, gfs, gfr, (0, 0), half)
     result = pltpu.make_async_copy(tg.at[me], out_hbm, wsem.at[0])
     result.start()
     bacc[...] = jnp.zeros_like(bacc)
@@ -421,7 +418,7 @@
     front, back_half = gk[:64], gk[64:]
     gk = jnp.concatenate([front * cost + back_half * sint, back_half * cost - front * sint], axis=0)
     gkv_out[...] = jnp.concatenate([gk.reshape(N_T, 8, TOK), gv.reshape(N_T, 8, TOK)], axis=1).astype(bf16)
-    for rel in PEERS[::-1]:
+    for rel in FAR:
         i = ridx(rel)
         to = peer(me, rel)
         send(gkv_out.at[to], gkv_in.at[me], ks.at[i], kr.at[i], to)
@@ -453,7 +450,7 @@
 
     lax.fori_loop(0, N_T, key_step, 0, unroll=4)
     gnv_in[me] = gnv[me]
-    for rel in PEERS:
+    for rel in FAR:
         i = ridx(rel)
         to = peer(me, rel)
         send(gnv.at[to], gnv_in.at[me], ns.at[i], nr.at[i], to)
@@ -462,7 +459,7 @@
         arrived(gnv_in.at[source(me, rel)], ns.at[i], nr.at[i])
     dpv[...] = jnp.sum(gnv_in[...], axis=0)
     dpv_in[dp] = dpv[...]
-    for d in range(1, N_DP):
+    for d in (5, 3, 4, 2, 6, 7, 1):
         send(dpv, dpv_in.at[dp], ds.at[d], dr.at[d], me, (dp + d) % N_DP)
     for d in range(1, N_DP):
         arrived(dpv_in.at[(dp + N_DP - d) % N_DP], ds.at[d], dr.at[d])
@@ -521,7 +518,7 @@
             vm((8, TOK, SHARD), bf16),
             vm((8, TOK, SHARD), bf16),
             vm((8, TOK, SHARD), bf16),
-            vm((len(SUMS), 128, SHARD), bf16),
+            vm((len(SUMS), 144, SHARD), bf16),
             vm((N_T, TOK, SHARD), bf16),
             vm((TOK, SHARD), f32),
             vm((TOK, SHARD), bf16),

time: 101 us -> 97.9 us (0.969)
  Pallas kernels: 100 us -> 97.2 us
    pallas_call x1, Pallas kernels: 98.6 us -> 95.5 us  [whole(): pl.pallas_call(body, name='block', out_shape=[sds((TOK, SHARD), bf16), sd...]
where the time goes in v5:
time: 97.9 us; the launch traced here: 97.8 us
  Pallas kernels  97.2 us (99%)
    pallas_call x1, Pallas kernels, whole(): pl.pallas_call(body, name='block', out_shape=[sds((TOK, SHARD), bf16), sd...  95.5 us

profile of v5, /device:TPU:0, one launch (start us, length us, event | category | flops | bytes accessed | tf_op | source)
XLA Modules:
  0.0 97.8 jit_solution(2457197764975573020)
XLA Ops:
  0.6 95.5 %block.1 = (bf16[256,512]{1,0:T(8,128)(2,1)}, f32[4,128]{1,0:T(4,128)}) custom-call(bf16[256,512]{1,0:T(8,128)(2,1)} %x_hbm.1, f32[1,8192]{1,0:T(1,128)} %bitcast.9, f32[1,8192]{1,0:T(1,128)} %bitcast.10, s32[1,8192]{1,0:T(1,128)} %bitcast.11, f32[1,8192]{1,0:T(1,128)} %bitcast.12, s32[1,256]{1,0:T(1,128)} %doc_hbm.1, f32[256,128]{1,0:T(8,128)} %constant.8.clone.cos_hbm, ...), custom_call_target="tpu_custom_call" | custom-call | tf_op jit(solution)/shard_map/block/pallas_call | solution.py:480
  96.1 1.7 %finish.1 = (bf16[256,512]{1,0:T(8,128)(2,1)}, f32[4,128]{1,0:T(4,128)}) custom-call(bf16[256,512]{1,0:T(8,128)(2,1)} %get-tuple-element.6.shard_ref, f32[4,128]{1,0:T(4,128)} %get-tuple-element.7.gn_ref), custom_call_target="tpu_custom_call" | custom-call | tf_op jit(solution)/shard_map/finish/pallas_call | solution.py:546

commit v6 on v5

--- a/solution.py
+++ b/solution.py
@@ -43,8 +43,10 @@
     ([1], [], [((1, 0), 0)]),
     ([4], [8], [((0, 3), 1)]),
     ([5], [9], [((0, 1), 1)]),
-    ([6, 7], [16, 17], [((0, 2), 0)]),
-    ([12, 13], [14, 15], [((1, 3), 1), ((1, 1), 1)]),
+    ([6], [16], []),
+    ([7], [17], [((0, 2), 0)]),
+    ([12], [14], [((1, 3), 1)]),
+    ([13], [15], [((1, 1), 1)]),
     ([8, 9], [], [((0, 2), 1)]),
     ([10, 11], [], [((1, 3), 0), ((1, 1), 0)]),
     ([14, 15], [], [((1, 2), 1)]),
@@ -133,7 +135,7 @@
         pltpu.make_async_copy(wq_hbm, wq, wsem.at[2]),
         pltpu.make_async_copy(wo_hbm, wo, wsem.at[3]),
     ]
-    for load in loads:
+    for load in loads[:2]:
         load.start()
 
     sends = []
@@ -255,6 +257,8 @@
         scale = lax.rsqrt(total / WIDTH + EPSILON)
         rs[...] = jnp.transpose(jnp.broadcast_to(scale[0:1, :], (128, TOK)))
 
+        for load in loads[2:]:
+            load.start()
         for load in loads[:2]:
             load.wait()
 
@@ -280,7 +284,11 @@
         return carry
 
     loads[2].wait()
+    early = len(sends) - len(PEERS)
     lax.fori_loop(0, N_T // 4, query_four, 0)
+    for cp in sends[:early]:
+        cp.wait_send()
+    del sends[:early]
     for h in range(HEADS):
         cut = slice(h * 128, h * 128 + 128)
         for out, top in ((qp, 0), (qt, TOK)):
@@ -423,6 +431,7 @@
         to = peer(me, rel)
         send(gkv_out.at[to], gkv_in.at[me], ks.at[i], kr.at[i], to)
     gkv_in[me] = gkv_out[me]
+    early = len(sends) - len(PEERS)
     for h in range(HEADS):
         cut = slice(h * 128, h * 128 + 128)
         z = nt(marks[h], kp[...])
@@ -437,6 +446,9 @@
         return carry
 
     lax.fori_loop(0, N_T, query_step, 0, unroll=4)
+    for cp in sends[:early]:
+        cp.wait_send()
+    del sends[:early]
     for rel in PEERS:
         i = ridx(rel)
         arrived(gkv_in.at[source(me, rel)], ks.at[i], kr.at[i])
@@ -448,12 +460,19 @@
         gnv[j] += column_sums(dot(gkv[...], wkv[:, lanes_of(j)]) * slopes[j])
         return carry
 
-    lax.fori_loop(0, N_T, key_step, 0, unroll=4)
+    for group in (FAR[:8], FAR[8:]):
+        for rel in group:
+            key_step(peer(me, rel), 0)
+        for rel in group:
+            i = ridx(rel)
+            to = peer(me, rel)
+            send(gnv.at[to], gnv_in.at[me], ns.at[i], nr.at[i], to)
+    key_step(me, 0)
     gnv_in[me] = gnv[me]
-    for rel in FAR:
-        i = ridx(rel)
-        to = peer(me, rel)
-        send(gnv.at[to], gnv_in.at[me], ns.at[i], nr.at[i], to)
+    early = len(sends) - len(PEERS)
+    for cp in sends[:early]:
+        cp.wait_send()
+    del sends[:early]
     for rel in PEERS:
         i = ridx(rel)
         arrived(gnv_in.at[source(me, rel)], ns.at[i], nr.at[i])
@@ -461,10 +480,14 @@
     dpv_in[dp] = dpv[...]
     for d in (5, 3, 4, 2, 6, 7, 1):
         send(dpv, dpv_in.at[dp], ds.at[d], dr.at[d], me, (dp + d) % N_DP)
+    early = len(sends) - N_DP + 1
+    for cp in sends[:early]:
+        cp.wait_send()
+    del sends[:early]
+    result.wait()
     for d in range(1, N_DP):
         arrived(dpv_in.at[(dp + N_DP - d) % N_DP], ds.at[d], dr.at[d])
     gn_ref[...] = jnp.sum(dpv_in[...], axis=0)[0:4, :]
-    result.wait()
     for cp in sends:
         cp.wait_send()
 

time: 97.9 us -> 96.1 us (0.982)
  Pallas kernels: 97.2 us -> 95.3 us
    pallas_call x1, Pallas kernels: 95.5 us -> 93.6 us  [whole(): pl.pallas_call(body, name='block', out_shape=[sds((TOK, SHARD), bf16), sd...]
where the time goes in v6:
time: 96.1 us; the launch traced here: 95.9 us
  Pallas kernels  95.3 us (99%)
    pallas_call x1, Pallas kernels, whole(): pl.pallas_call(body, name='block', out_shape=[sds((TOK, SHARD), bf16), sd...  93.6 us

profile of v6, /device:TPU:0, one launch (start us, length us, event | category | flops | bytes accessed | tf_op | source)
XLA Modules:
  0.0 95.9 jit_solution(15005966884640266081)
XLA Ops:
  0.6 93.6 %block.1 = (bf16[256,512]{1,0:T(8,128)(2,1)}, f32[4,128]{1,0:T(4,128)}) custom-call(bf16[256,512]{1,0:T(8,128)(2,1)} %x_hbm.1, f32[1,8192]{1,0:T(1,128)} %bitcast.9, f32[1,8192]{1,0:T(1,128)} %bitcast.10, s32[1,8192]{1,0:T(1,128)} %bitcast.11, f32[1,8192]{1,0:T(1,128)} %bitcast.12, s32[1,256]{1,0:T(1,128)} %doc_hbm.1, f32[256,128]{1,0:T(8,128)} %constant.8.clone.cos_hbm, ...), custom_call_target="tpu_custom_call" | custom-call | tf_op jit(solution)/shard_map/block/pallas_call | solution.py:503
  94.3 1.7 %finish.1 = (bf16[256,512]{1,0:T(8,128)(2,1)}, f32[4,128]{1,0:T(4,128)}) custom-call(bf16[256,512]{1,0:T(8,128)(2,1)} %get-tuple-element.6.shard_ref, f32[4,128]{1,0:T(4,128)} %get-tuple-element.7.gn_ref), custom_call_target="tpu_custom_call" | custom-call | tf_op jit(solution)/shard_map/finish/pallas_call | solution.py:569

commit v7 on v6

--- a/solution.py
+++ b/solution.py
@@ -25,6 +25,7 @@
 HEADS = 4
 N_DP = 8
 VMEM_BYTES = 60 << 20
+HALF = TOK // 2
 
 RELS = [(dy, dz, dc) for dy in range(N_Y) for dz in range(N_Z) for dc in range(N_C)]
 PEERS = [r for r in RELS if r != (0, 0, 0)]
@@ -310,9 +311,13 @@
         out[0:64, :] = (front * cost - back * sint).astype(bf16)
         out[64:128, :] = (back * cost + front * sint).astype(bf16)
 
-    same = jnp.concatenate([docs[...], docs[...]], axis=1) == doc_ref[...].astype(f32)
-    place = lax.broadcasted_iota(jnp.int32, (TOK, TOK), 0) >= lax.broadcasted_iota(jnp.int32, (TOK, TOK), 1)
-    allowed = same & place
+    def allowed(t):
+        n = HALF * (t + 1)
+        same = jnp.concatenate([docs[pl.ds(t * HALF, HALF), :]] * (t + 1), axis=1) == doc_ref[:, 0:n].astype(f32)
+        row = lax.broadcasted_iota(jnp.int32, (HALF, n), 0) + t * HALF
+        return same & (row >= lax.broadcasted_iota(jnp.int32, (HALF, n), 1))
+
+    masks = [allowed(0), allowed(1)]
     score_scale = HEAD_DIM ** (-0.5)
 
     def dot(a, b):
@@ -320,14 +325,17 @@
 
     for h in range(HEADS):
         cut = slice(h * 128, h * 128 + 128)
-        q0, q1 = qp[:, cut], qt[:, cut]
-        scores = jnp.where(allowed, dot(q0, kp[...]) * score_scale, MASKED)
-        grown = jnp.exp(scores - jnp.max(scores, axis=1, keepdims=True))
-        prob = grown / jnp.sum(grown, axis=1, keepdims=True)
-        probs[h] = prob
-        t = (dot(q1, kp[...]) + dot(q0, kt[...])) * score_scale
-        tan = (prob * (t - jnp.sum(prob * t, axis=1, keepdims=True))).astype(bf16)
-        ctx[:, cut] = (nt(tan, vp[...]) + nt(prob.astype(bf16), vt[...])).astype(bf16)
+        for t in range(2):
+            rows, n = pl.ds(t * HALF, HALF), HALF * (t + 1)
+            q0, q1 = qp[rows, cut], qt[rows, cut]
+            k0 = kp[:, 0:n]
+            scores = jnp.where(masks[t], dot(q0, k0) * score_scale, MASKED)
+            grown = jnp.exp(scores - jnp.max(scores, axis=1, keepdims=True))
+            prob = grown / jnp.sum(grown, axis=1, keepdims=True)
+            probs[h, rows, 0:n] = prob
+            tan = (dot(q1, k0) + dot(q0, kt[:, 0:n])) * score_scale
+            tan = (prob * (tan - jnp.sum(prob * tan, axis=1, keepdims=True))).astype(bf16)
+            ctx[rows, cut] = (nt(tan, vp[:, 0:n]) + nt(prob.astype(bf16), vt[:, 0:n])).astype(bf16)
 
     loads[3].wait()
 
@@ -411,18 +419,21 @@
 
     gather(tg, gs, gr, gfs, gfr, lambda j, half: None, back, None)
 
-    gk = jnp.zeros((HEAD_DIM, TOK), f32)
-    gv = jnp.zeros((HEAD_DIM, TOK), f32)
-    marks = []
+    gk = [jnp.zeros((HEAD_DIM, HALF * (t + 1)), f32) for t in range(2)]
+    gv = [jnp.zeros((HEAD_DIM, HALF * (t + 1)), f32) for t in range(2)]
+    marks = {}
     for h in range(HEADS):
         cut = slice(h * 128, h * 128 + 128)
-        bc = bacc[:, cut].astype(bf16)
-        prob = probs[h]
-        g = dot(bc, vp[...])
-        score = (prob * (g - jnp.sum(prob * g, axis=1, keepdims=True)) * score_scale).astype(bf16)
-        marks.append(score)
-        gk = gk + tn(qp[:, cut], score)
-        gv = gv + tn(bc, prob.astype(bf16))
+        for t in range(2):
+            rows, n = pl.ds(t * HALF, HALF), HALF * (t + 1)
+            bc = bacc[rows, cut].astype(bf16)
+            prob = probs[h, rows, 0:n]
+            g = dot(bc, vp[:, 0:n])
+            score = (prob * (g - jnp.sum(prob * g, axis=1, keepdims=True)) * score_scale).astype(bf16)
+            marks[h, t] = score
+            gk[t] = gk[t] + tn(qp[rows, cut], score)
+            gv[t] = gv[t] + tn(bc, prob.astype(bf16))
+    gk, gv = (jnp.concatenate([v[0] + v[1][:, :HALF], v[1][:, HALF:]], axis=1) for v in (gk, gv))
     front, back_half = gk[:64], gk[64:]
     gk = jnp.concatenate([front * cost + back_half * sint, back_half * cost - front * sint], axis=0)
     gkv_out[...] = jnp.concatenate([gk.reshape(N_T, 8, TOK), gv.reshape(N_T, 8, TOK)], axis=1).astype(bf16)
@@ -434,8 +445,10 @@
     early = len(sends) - len(PEERS)
     for h in range(HEADS):
         cut = slice(h * 128, h * 128 + 128)
-        z = nt(marks[h], kp[...])
-        gq[:, cut] = (z * cos_ref[...] - pltpu.roll(z, 64, 1) * sin_ref[...]).astype(bf16)
+        for t in range(2):
+            rows = pl.ds(t * HALF, HALF)
+            z = nt(marks[h, t], kp[:, 0 : HALF * (t + 1)])
+            gq[rows, cut] = (z * cos_ref[rows, :] - pltpu.roll(z, 64, 1) * sin_ref[rows, :]).astype(bf16)
 
     def column_sums(product):
         line = jnp.sum(product, axis=0, keepdims=True)

time: 96.1 us -> 97 us (level)
  no operation moved by 1% of the time
where the time goes in v7:
time: 97 us; the launch traced here: 96.9 us
  Pallas kernels  96.2 us (99%)
    pallas_call x1, Pallas kernels, whole(): pl.pallas_call(body, name='block', out_shape=[sds((TOK, SHARD), bf16), sd...  94.6 us

profile of v7, /device:TPU:0, one launch (start us, length us, event | category | flops | bytes accessed | tf_op | source)
XLA Modules:
  0.0 96.9 jit_solution(10611378917082585701)
XLA Ops:
  0.6 94.6 %block.1 = (bf16[256,512]{1,0:T(8,128)(2,1)}, f32[4,128]{1,0:T(4,128)}) custom-call(bf16[256,512]{1,0:T(8,128)(2,1)} %x_hbm.1, f32[1,8192]{1,0:T(1,128)} %bitcast.9, f32[1,8192]{1,0:T(1,128)} %bitcast.10, s32[1,8192]{1,0:T(1,128)} %bitcast.11, f32[1,8192]{1,0:T(1,128)} %bitcast.12, s32[1,256]{1,0:T(1,128)} %doc_hbm.1, f32[256,128]{1,0:T(8,128)} %constant.8.clone.cos_hbm, ...), custom_call_target="tpu_custom_call" | custom-call | tf_op jit(solution)/shard_map/block/pallas_call | solution.py:516
  95.2 1.7 %finish.1 = (bf16[256,512]{1,0:T(8,128)(2,1)}, f32[4,128]{1,0:T(4,128)}) custom-call(bf16[256,512]{1,0:T(8,128)(2,1)} %get-tuple-element.6.shard_ref, f32[4,128]{1,0:T(4,128)} %get-tuple-element.7.gn_ref), custom_call_target="tpu_custom_call" | custom-call | tf_op jit(solution)/shard_map/finish/pallas_call | solution.py:582
